TPU v7x, 256 devices: a whole 4x4x8 slice. The times are simulated.
256 devices in a mesh: lat: 16 (over x, y_hi, core), lon: 16 (over y_lo, z).
Axes of the slice: x: 4, y: 4 (y_hi: 2, y_lo: 2; y = y_hi * 2 + y_lo), z: 8, core: 2. Of those that a mesh axis runs over, the one named last changes fastest.
Arguments:
- tokens: bfloat16 [4, 192, 192, 192], P(None, 'lat', 'lon'), may hold values from -6 to 6
- cotangent: bfloat16 [4, 192, 192, 192], P(None, 'lat', 'lon'), may hold values from -6 to 6
- w_qkv: bfloat16 [2, 192, 576], replicated, may hold values from -0.4375 to 0.4375
- w_proj: bfloat16 [2, 192, 192], replicated, may hold values from -0.4375 to 0.4375
- w_in: bfloat16 [2, 192, 768], replicated, may hold values from -0.4375 to 0.4375
- w_out: bfloat16 [2, 768, 192], replicated, may hold values from -0.21875 to 0.21875
- earth_bias: bfloat16 [2, 2, 32, 6, 20736], P(None, None, 'lat'), may hold values from -4 to 4
Outputs:
- d_tokens: bfloat16 [4, 192, 192, 192], P(None, 'lat', 'lon')
- d_qkv: float32 [2, 192, 576], replicated
- d_proj: float32 [2, 192, 192], replicated
- d_bias: float32 [2, 2, 32, 6, 20736], P(None, None, 'lat')
All inputs are finite; a program needn't handle non-finite values.
Results may differ from a plain program's by a relative error of at most 0.028.
Values may be sent and summed in bfloat16 or wider, within the bound.
A program may use at most 128 MiB of HBM per device.

v0:
```python
import functools

import jax
import jax.numpy as jnp
import numpy as np
from jax import lax
from jax.experimental import pallas as pl
from jax.experimental.pallas import tpu as pltpu
from jax.sharding import PartitionSpec as P

F32 = jnp.float32
BF16 = jnp.bfloat16
C = 192
HEADS = 6
HD = 32
FF = 768
WIN = 144
TOK = 576
EPSILON = 1e-05
SCALE = HD ** (-0.5)
MESH = pl.DeviceIdType.MESH
E0, S0, D0, SEND = 0, 224, 304, 384
ONCE = pl.Buffered(1)
VMEM_LIMIT = 56 * 1024 * 1024


def _plain_index(level, row, col):
    window = (level // 2) * 2 + row // 6
    return window * WIN + (level % 2) * 72 + (row % 6) * 12 + col


def _matrices():
    load = np.zeros((TOK, 768), np.float32)
    own = np.zeros((TOK, TOK), np.float32)
    send = np.zeros((SEND, TOK), np.float32)
    recv = np.zeros((TOK, SEND), np.float32)
    for level in range(4):
        for row in range(12):
            for col in range(12):
                here = _plain_index(level, row, col)
                load[here, (level * 12 + row) * 16 + col] = 1
                target_row, target_col = row - 3, col - 6
                target = _plain_index((level - 1) % 4, target_row % 12, target_col % 12)
                if target_row >= 0 and target_col >= 0:
                    own[target, here] = 1
                    continue
                if target_row >= 0:
                    slot = E0 + (level * 9 + row - 3) * 6 + col
                elif target_col >= 0:
                    slot = S0 + (level * 3 + row) * 6 + col - 6
                else:
                    slot = D0 + (level * 3 + row) * 6 + col
                send[slot, here] = 1
                recv[target, slot] = 1
    return load, own, send, recv


def nn(a, b):
    return jnp.dot(a, b, preferred_element_type=F32)


def nt(a, b):
    return lax.dot_general(a, b, (((1,), (1,)), ((), ())), preferred_element_type=F32)


def eye(n):
    rows = lax.broadcasted_iota(jnp.int32, (n, n), 0)
    cols = lax.broadcasted_iota(jnp.int32, (n, n), 1)
    return jnp.where(rows == cols, 1.0, 0.0).astype(BF16)


def flip(a, n):
    return nt(eye(n), a).astype(BF16)


def normalize(x):
    center = jnp.mean(x, axis=-1, keepdims=True)
    offset = x - center
    spread = jnp.mean(offset * offset, axis=-1, keepdims=True)
    inverse = lax.rsqrt(spread + EPSILON)
    return offset * inverse, inverse


def norm_back(x, upstream):
    normed, inverse = normalize(x)
    first = jnp.mean(upstream, axis=-1, keepdims=True)
    second = jnp.mean(upstream * normed, axis=-1, keepdims=True)
    return inverse * (upstream - first - normed * second)


def cumulative(x):
    return 0.5 * (1.0 + lax.erf(x * 0.7071067811865476))


def density(x):
    return 0.3989422804014327 * jnp.exp(-0.5 * x * x)


def rows_of(window):
    return pl.ds(pl.multiple_of(window * WIN, WIN), WIN)


def spread_bias(bias_ref, window, main, rest):
    def step(group, carry):
        block = bias_ref[
            0, window // 2, window % 2, :, pl.ds(pl.multiple_of(group * 1152, 128), 1152)
        ].astype(F32)
        for r in range(8):
            at = pl.ds(pl.multiple_of(group * 64, 64) + 8 * r, 6)
            main[at, :] = block[:, WIN * r : WIN * r + 128]
            rest[at, 0:16] = block[:, WIN * r + 128 : WIN * r + WIN]
        return carry

    lax.fori_loop(0, 18, step, 0)


def head_bias(main, rest, head):
    left = main[pl.ds(head, WIN, stride=8), :]
    right = rest[pl.ds(head, WIN, stride=8), :]
    return jnp.concatenate([left, right[:, :16]], axis=1)


def attention_forward(window, qkv_ref, qkvt_ref, prob_ref, mixedt_ref, mixed_ref, bias_ref, main, rest, mask):
    qkv = qkv_ref[rows_of(window), :]
    qkvt_ref[window] = flip(qkv, 3 * C)
    spread_bias(bias_ref, window, main, rest)
    for head in range(HEADS):
        lo = head * HD
        keys = qkvt_ref[window, C + lo : C + lo + HD, :]
        values = qkvt_ref[window, 2 * C + lo : 2 * C + lo + HD, :]
        scores = nn(qkv[:, lo : lo + HD], keys) * SCALE + head_bias(main, rest, head)
        weights = jnp.exp(scores)
        if mask is not None:
            weights = weights * mask
        probs = weights / jnp.sum(weights, axis=-1, keepdims=True)
        prob_ref[window * HEADS + head] = probs
        mixedt_ref[window, lo : lo + HD, :] = nt(values, probs.astype(BF16)).astype(BF16)
    mixed_ref[rows_of(window), :] = flip(mixedt_ref[window], WIN)


def attention_backward(
    window, source_ref, qkv_ref, qkvt_ref, prob_ref, mixedt_ref, mgrad_ref, grad_ref,
    w_qkv, w_proj, gradt, sgrad_ref, wgrad, main, rest,
):
    mgrad = mgrad_ref[rows_of(window), :]
    wgrad[:, 3 * C :] += nn(mixedt_ref[window], mgrad)
    grad = grad_ref[rows_of(window), :]
    gt = nt(w_proj, mgrad).astype(BF16)
    for head in range(HEADS):
        lo = head * HD
        queries = qkvt_ref[window, lo : lo + HD, :]
        keys = qkvt_ref[window, C + lo : C + lo + HD, :]
        values = qkvt_ref[window, 2 * C + lo : 2 * C + lo + HD, :]
        probs = prob_ref[window * HEADS + head]
        pgrad = nn(grad[:, lo : lo + HD], values)
        vgrad = nn(gt[lo : lo + HD, :], probs.astype(BF16))
        delta = jnp.sum(pgrad * probs, axis=-1, keepdims=True)
        sgrad = probs * (pgrad - delta)
        at = pl.ds(window * HEADS + head, WIN, stride=24)
        main[at, :] = sgrad[:, :128]
        rest[at, :] = jnp.concatenate([sgrad[:, 128:], jnp.zeros((WIN, 112), F32)], axis=1)
        sround = sgrad.astype(BF16)
        gradt[lo : lo + HD, :] = (nt(keys, sround) * SCALE).astype(BF16)
        gradt[C + lo : C + lo + HD, :] = (nn(queries, sround) * SCALE).astype(BF16)
        gradt[2 * C + lo : 2 * C + lo + HD, :] = vgrad.astype(BF16)
    all_grad = gradt[...]
    sourcet = flip(source_ref[rows_of(window), :], C)
    wgrad[:, : 3 * C] += nt(sourcet, all_grad)
    sgradt = nn(w_qkv, all_grad).astype(BF16)
    sgrad_ref[rows_of(window), :] = flip(sgradt, WIN)


def pack_bias(main, rest, out_ref):
    def flat(first):
        parts = []
        for r in range(8):
            at = pl.ds(pl.multiple_of(first * 192, 8) + 24 * r, 24)
            parts += [main[at, :], rest[at, :][:, :16]]
        return jnp.concatenate(parts, axis=1)

    def step(group, carry):
        top = flat(group)
        bottom = flat(group + 9)
        for third in range(3):
            both = jnp.concatenate(
                [top[8 * third : 8 * third + 8], bottom[8 * third : 8 * third + 8]], axis=0
            ).astype(BF16)
            for j in range(9):
                out_ref[third * 81 + group * 9 + j] = both[:, 128 * j : 128 * j + 128]
        return carry

    lax.fori_loop(0, 9, step, 0)
    out_ref[243:256] = jnp.zeros((13, 16, 128), BF16)


def pack_weights(wgrad, out_ref):
    for i in range(12):
        block = wgrad[16 * i : 16 * i + 16, :].astype(BF16)
        for j in range(6):
            out_ref[6 * i + j] = block[:, 128 * j : 128 * j + 128]


def mlp_back(middle, upstream, slope, w_in, w_out):
    act_grad = nt(upstream, w_out)
    pre_grad = (slope * act_grad).astype(BF16)
    ngrad = nt(pre_grad, w_in)
    return (upstream.astype(F32) + norm_back(middle.astype(F32), ngrad)).astype(BF16)


def load_grid(grid_ref, pad, matrix):
    for i in range(48):
        pad[16 * i : 16 * i + 12, :] = grid_ref[i]
    return nn(matrix, pad[...]).astype(BF16)


def forward_kernel(
    tok_ref, cot_ref, load_ref, own_ref, send_ref, w_qkv, w_proj, w_in, w_out, bias_ref,
    x_out, source_out, qkv_out, qkvt_out, prob_out, mixedt_out, mid_out, slope_out, kept_out, sent_out,
    pad, mixed, main, rest,
):
    pad[...] = jnp.zeros_like(pad)
    cot = load_grid(cot_ref, pad, load_ref[...])
    kept_out[1] = nn(own_ref[...], cot).astype(BF16)
    sent_out[1] = nn(send_ref[...], cot).astype(BF16)
    x = load_grid(tok_ref, pad, load_ref[...])
    x_out[...] = x
    x = x.astype(F32)
    source = normalize(x)[0].astype(BF16)
    source_out[...] = source
    qkv_out[...] = nn(source, w_qkv[0]).astype(BF16)

    def step(window, carry):
        attention_forward(
            window, qkv_out, qkvt_out, prob_out, mixedt_out, mixed, bias_ref, main, rest, None
        )
        return carry

    lax.fori_loop(0, 4, step, 0)
    attended = nn(mixed[...], w_proj[0]).astype(BF16)
    middle = (x + attended.astype(F32)).astype(BF16)
    mid_out[...] = middle
    middle = middle.astype(F32)
    pre = nn(normalize(middle)[0].astype(BF16), w_in[0])
    phi = cumulative(pre)
    slope_out[...] = phi + pre * density(pre)
    hidden = (pre * phi).astype(BF16)
    x1 = (middle + nn(hidden, w_out[0])).astype(BF16)
    kept_out[0] = nn(own_ref[...], x1).astype(BF16)
    sent_out[0] = nn(send_ref[...], x1).astype(BF16)


def region_mask(window):
    last_lat = lax.axis_index("lat") == lax.axis_size("lat") - 1

    def region(tokens):
        level = tokens // 72
        row = tokens // 12 % 6
        upper = jnp.where(window // 2 == 1, level, 0)
        lower = jnp.where(jnp.logical_and(last_lat, window % 2 == 1), row // 3, 0)
        return upper * 2 + lower

    queries = region(lax.broadcasted_iota(jnp.int32, (WIN, WIN), 0))
    keys = region(lax.broadcasted_iota(jnp.int32, (WIN, WIN), 1))
    return jnp.where(queries == keys, 1.0, 0.0)


def middle_kernel(
    kept_ref, arrived_ref, recv_ref, send2_ref, own2_ref, w_qkv, w_proj, w_in, w_out, bias_ref,
    kept_out, sent_out, tiles_out, wtiles_out,
    source, qkv, qkvt, prob, mixedt, mixed, mgrad, grad, gradt, sgrad, wgrad, main, rest, main24, rest24,
):
    x = (kept_ref[0].astype(F32) + nn(recv_ref[...], arrived_ref[0])).astype(BF16)
    cot = (kept_ref[1].astype(F32) + nn(recv_ref[...], arrived_ref[1])).astype(BF16)
    x = x.astype(F32)
    source[...] = normalize(x)[0].astype(BF16)
    qkv[...] = nn(source[...], w_qkv[0]).astype(BF16)

    def step(window, carry):
        attention_forward(
            window, qkv, qkvt, prob, mixedt, mixed, bias_ref, main, rest, region_mask(window)
        )
        return carry

    lax.fori_loop(0, 4, step, 0)
    attended = nn(mixed[...], w_proj[0]).astype(BF16)
    middle = (x + attended.astype(F32)).astype(BF16)
    pre = nn(normalize(middle.astype(F32))[0].astype(BF16), w_in[0])
    slope = cumulative(pre) + pre * density(pre)
    mgrad[...] = mlp_back(middle, cot, slope, w_in[0], w_out[0])
    grad[...] = nt(mgrad[...], w_proj[0]).astype(BF16)
    wgrad[...] = jnp.zeros_like(wgrad)

    def back(window, carry):
        attention_backward(
            window, source, qkv, qkvt, prob, mixedt, mgrad, grad, w_qkv[0], w_proj[0], gradt, sgrad,
            wgrad, main24, rest24,
        )
        return carry

    lax.fori_loop(0, 4, back, 0)
    result = (mgrad[...].astype(F32) + norm_back(x, sgrad[...].astype(F32))).astype(BF16)
    kept_out[...] = nn(own2_ref[...], result).astype(BF16)
    sent_out[...] = nn(send2_ref[...], result).astype(BF16)
    pack_bias(main24, rest24, tiles_out)
    pack_weights(wgrad, wtiles_out)


def backward_kernel(
    kept_ref, arrived_ref, recv2_ref, loadt_ref, x_ref, source_ref, qkv_ref, qkvt_ref, prob_ref, mixedt_ref,
    mid_ref, slope_ref, w_qkv, w_proj, w_in, w_out,
    grid_out, tiles_out, wtiles_out,
    mgrad, grad, gradt, sgrad, wgrad, main24, rest24,
):
    upstream = (kept_ref[...].astype(F32) + nn(recv2_ref[...], arrived_ref[...])).astype(BF16)
    mgrad[...] = mlp_back(mid_ref[...], upstream, slope_ref[...], w_in[0], w_out[0])
    grad[...] = nt(mgrad[...], w_proj[0]).astype(BF16)
    wgrad[...] = jnp.zeros_like(wgrad)

    def back(window, carry):
        attention_backward(
            window, source_ref, qkv_ref, qkvt_ref, prob_ref, mixedt_ref, mgrad, grad, w_qkv[0], w_proj[0],
            gradt, sgrad, wgrad, main24, rest24,
        )
        return carry

    lax.fori_loop(0, 4, back, 0)
    x = x_ref[...].astype(F32)
    result = (mgrad[...].astype(F32) + norm_back(x, sgrad[...].astype(F32))).astype(BF16)
    placed = nn(loadt_ref[...], result).astype(BF16)
    for i in range(48):
        grid_out[i] = placed[16 * i : 16 * i + 12, :]
    pack_bias(main24, rest24, tiles_out)
    pack_weights(wgrad, wtiles_out)


def whole(ndim):
    return lambda *_: (0,) * ndim


def compute_call(kernel, operands, outs, scratch):
    specs, arrays = [], []
    for operand in operands:
        array, layer = operand if isinstance(operand, tuple) else (operand, None)
        arrays.append(array)
        shape = array.shape if layer is None else (1,) + array.shape[1:]
        index = (0 if layer is None else layer,) + (0,) * (array.ndim - 1)
        specs.append(pl.BlockSpec(shape, functools.partial(lambda at, _: at, index), pipeline_mode=ONCE))
    return pl.pallas_call(
        kernel,
        out_shape=[jax.ShapeDtypeStruct(shape, kind) for shape, kind in outs],
        in_specs=specs,
        out_specs=[pl.BlockSpec(shape, whole(len(shape)), pipeline_mode=ONCE) for shape, kind in outs],
        grid=(1,),
        scratch_shapes=[pltpu.VMEM(shape, kind) for shape, kind in scratch],
        compiler_params=pltpu.CompilerParams(vmem_limit_bytes=VMEM_LIMIT),
    )(*arrays)


def neighbour(lat_steps, lon_steps):
    lats, lons = lax.axis_size("lat"), lax.axis_size("lon")
    return (
        lax.rem(lax.axis_index("lat") + lat_steps + lats, lats),
        lax.rem(lax.axis_index("lon") + lon_steps + lons, lons),
    )


def exchange_kernel(sign, send_ref, out_ref, send_sems, recv_sems):
    barrier = pltpu.get_barrier_semaphore()
    steps = [(0, sign, E0, S0), (sign, 0, S0, D0), (sign, sign, D0, SEND)]
    for lat, lon, _, _ in steps:
        pl.semaphore_signal(barrier, inc=1, device_id=neighbour(-lat, -lon), device_id_type=MESH)
    pl.semaphore_wait(barrier, 3)
    copies = []
    for i, (lat, lon, start, stop) in enumerate(steps):
        piece = pl.ds(start, stop - start)
        copy = pltpu.make_async_remote_copy(
            src_ref=send_ref.at[:, piece],
            dst_ref=out_ref.at[:, piece],
            send_sem=send_sems.at[i],
            recv_sem=recv_sems.at[i],
            device_id=neighbour(lat, lon),
            device_id_type=MESH,
        )
        copy.start()
        copies.append(copy)
    for copy in copies:
        copy.wait()


def exchange(sent, sign, collective_id):
    return pl.pallas_call(
        functools.partial(exchange_kernel, sign),
        out_shape=jax.ShapeDtypeStruct(sent.shape, BF16),
        in_specs=[pl.BlockSpec(memory_space=pltpu.VMEM)],
        out_specs=pl.BlockSpec(memory_space=pltpu.VMEM),
        scratch_shapes=[pltpu.SemaphoreType.DMA((3,)), pltpu.SemaphoreType.DMA((3,))],
        compiler_params=pltpu.CompilerParams(collective_id=collective_id, has_side_effects=True),
    )(sent)


ZS = 8
CHUNK = 32


def reduce_kernel(
    tiles0, tiles1, w0, w1, out_ref, wout_ref,
    right_in, left_in, right_sum, left_sum, mine, other, wpart, wmid, wown, w_all,
    rs_send, rs_recv, ls_send, ls_recv, y_send, y_recv, ga_send, ga_recv, gb_send, gb_recv,
    wa_send, wa_recv, wb_send, wb_recv, wc_send, wc_recv, wd_send, wd_recv,
):
    lat = lax.axis_index("lat")
    lon = lax.axis_index("lon")
    z = lax.rem(lon, ZS)
    y = lon // ZS
    lats = lax.axis_size("lat")
    lons = lax.axis_size("lon")

    def along(steps):
        return (lat, y * ZS + lax.rem(z + steps + ZS, ZS))

    def copy_to(src, dst, send, recv, device):
        return pltpu.make_async_remote_copy(
            src_ref=src, dst_ref=dst, send_sem=send, recv_sem=recv, device_id=device, device_id_type=MESH
        )

    barrier = pltpu.get_barrier_semaphore()
    for k in range(1, 16):
        pl.semaphore_signal(barrier, inc=1, device_id=(lax.rem(lat + k, lats), lon), device_id_type=MESH)
        pl.semaphore_signal(barrier, inc=1, device_id=(lat, lax.rem(lon + k, lons)), device_id_type=MESH)
    pl.semaphore_wait(barrier, 30)

    def own(tiles, owner):
        return tiles[pl.ds(lax.rem(owner + 2 * ZS, ZS) * CHUNK, CHUNK)]

    for layer, w in enumerate((w0, w1)):
        w_all[pl.ds(72 * layer, 72)] = w[...]
    started = []
    for k in range(1, 16):
        to = lax.rem(lat + k, lats)
        copy = copy_to(w_all.at[pl.ds(to * 9, 9)], wpart.at[k], wa_send.at[k], wa_recv.at[k], (to, lon))
        copy.start()
        started.append(copy)

    def ring_sum(step):
        for layer, tiles in enumerate((tiles0, tiles1)):
            value = own(tiles, z + 4 - step)
            if step:
                value = (value.astype(F32) + right_in[step - 1, layer].astype(F32)).astype(BF16)
            right_sum[step, layer] = value
            if step < 3:
                value = own(tiles, z - 3 + step)
                if step:
                    value = (value.astype(F32) + left_in[step - 1, layer].astype(F32)).astype(BF16)
                left_sum[step, layer] = value

    rings = []
    for step in range(4):
        if step:
            for copy in rings[-1]:
                copy.wait_recv()
        ring_sum(step)
        now = [copy_to(right_sum.at[step], right_in.at[step], rs_send.at[step], rs_recv.at[step], along(1))]
        if step < 3:
            now.append(
                copy_to(left_sum.at[step], left_in.at[step], ls_send.at[step], ls_recv.at[step], along(-1))
            )
        for copy in now:
            copy.start()
        rings.append(now)

    total = w_all[pl.ds(lat * 9, 9)].astype(F32)
    for k, copy in enumerate(started, 1):
        copy.wait_recv()
        total = total + wpart[k].astype(F32)
    wmid[0:9] = total.astype(BF16)
    for k in range(1, 16):
        to = lax.rem(lon + k, lons)

        @pl.when(to < 9)
        def _():
            copy_to(wmid.at[to], wown.at[k], wb_send.at[k], wb_recv.at[k], (lat, to)).start()

    rings[3][0].wait_recv()
    for layer, tiles in enumerate((tiles0, tiles1)):
        mine[layer] = (
            own(tiles, z).astype(F32) + right_in[3, layer].astype(F32) + left_in[2, layer].astype(F32)
        ).astype(BF16)
    swap = copy_to(mine, other, y_send.at[0], y_recv.at[0], (lat, (1 - y) * ZS + z))
    swap.start()

    @pl.when(lon < 9)
    def _():
        value = wmid[lon].astype(F32)
        for k in range(1, 16):
            copy_to(wmid.at[0], wown.at[k], wb_send.at[k], wb_recv.at[k], (lat, lon)).wait_recv()
            value = value + wown[k].astype(F32)
        wmid[9 + lon] = value.astype(BF16)
        for k in range(1, 16):
            to = lax.rem(lon + k, lons)
            copy_to(wmid.at[9 + lon], wmid.at[9 + lon], wc_send.at[k], wc_recv.at[k], (lat, to)).start()

    swap.wait_recv()
    for layer in range(2):
        out_ref[z, layer] = (mine[layer].astype(F32) + other[layer].astype(F32)).astype(BF16)

    gathers = []
    for step in range(4):
        if step:
            for copy in gathers[-1]:
                copy.wait_recv()
        at = lax.rem(z - step + ZS, ZS)
        now = [copy_to(out_ref.at[at], out_ref.at[at], ga_send.at[step], ga_recv.at[step], along(1))]
        if step < 3:
            at = lax.rem(z + step, ZS)
            now.append(copy_to(out_ref.at[at], out_ref.at[at], gb_send.at[step], gb_recv.at[step], along(-1)))
        for copy in now:
            copy.start()
        gathers.append(now)

        if step == 0:
            for k in range(1, 16):
                source = lax.rem(lon - k + lons, lons)

                @pl.when(source < 9)
                def _():
                    copy_to(
                        wmid.at[9 + source], wmid.at[9 + source], wc_send.at[k], wc_recv.at[k], (lat, source)
                    ).wait_recv()

            wout_ref[pl.ds(lat * 9, 9)] = wmid[9:18]
            final = []
            for k in range(1, 16):
                to = lax.rem(lat + k, lats)
                piece = wout_ref.at[pl.ds(lat * 9, 9)]
                copy = copy_to(piece, piece, wd_send.at[k], wd_recv.at[k], (to, lon))
                copy.start()
                final.append(copy)

    gathers[3][0].wait_recv()
    for copy in final:
        copy.wait()
    for now in rings + gathers:
        for copy in now:
            copy.wait_send()
    for copy in started:
        copy.wait_send()
    swap.wait_send()
    for k in range(1, 16):
        to = lax.rem(lon + k, lons)

        @pl.when(to < 9)
        def _():
            copy_to(wmid.at[to], wown.at[k], wb_send.at[k], wb_recv.at[k], (lat, to)).wait_send()

    @pl.when(lon < 9)
    def _():
        for k in range(1, 16):
            to = lax.rem(lon + k, lons)
            copy_to(wmid.at[9 + lon], wmid.at[9 + lon], wc_send.at[k], wc_recv.at[k], (lat, to)).wait_send()


def reduce_all(tiles0, tiles1, w0, w1):
    dma = pltpu.SemaphoreType.DMA
    ring = (2, CHUNK, 16, 128)
    scratch = [
        pltpu.VMEM((4,) + ring, BF16),
        pltpu.VMEM((3,) + ring, BF16),
        pltpu.VMEM((4,) + ring, BF16),
        pltpu.VMEM((3,) + ring, BF16),
        pltpu.VMEM(ring, BF16),
        pltpu.VMEM(ring, BF16),
        pltpu.VMEM((16, 9, 16, 128), BF16),
        pltpu.VMEM((18, 16, 128), BF16),
        pltpu.VMEM((16, 16, 128), BF16),
        pltpu.VMEM((144, 16, 128), BF16),
    ]
    sems = [4, 4, 3, 3, 1, 1, 4, 4, 3, 3] + [16] * 8
    return pl.pallas_call(
        reduce_kernel,
        out_shape=[
            jax.ShapeDtypeStruct((ZS,) + ring, BF16),
            jax.ShapeDtypeStruct((144, 16, 128), BF16),
        ],
        in_specs=[pl.BlockSpec(memory_space=pltpu.VMEM)] * 4,
        out_specs=[pl.BlockSpec(memory_space=pltpu.VMEM)] * 2,
        scratch_shapes=scratch + [dma((n,)) for n in sems],
        compiler_params=pltpu.CompilerParams(
            collective_id=2, has_side_effects=True, vmem_limit_bytes=VMEM_LIMIT
        ),
    )(tiles0, tiles1, w0, w1)


def unpack_kernel(tiles_ref, wtiles_ref, bias_out, qkv_out, proj_out):
    for j in range(81):
        rows = []
        for third in range(3):
            at = third * 81 + j
            rows.append(tiles_ref[at // CHUNK, 0, at % CHUNK].astype(F32))
        for half in range(2):
            full = jnp.concatenate([part[8 * half : 8 * half + 8] for part in rows], axis=0)
            lanes = slice(half * 10368 + 128 * j, half * 10368 + 128 * j + 128)
            for window in range(4):
                bias_out[0, window // 2, window % 2, :, lanes] = full[6 * window : 6 * window + 6]
    for i in range(12):
        row = jnp.concatenate([wtiles_ref[6 * i + j].astype(F32) for j in range(6)], axis=1)
        qkv_out[0, 16 * i : 16 * i + 16, :] = row[:, : 3 * C]
        proj_out[0, 16 * i : 16 * i + 16, :] = row[:, 3 * C :]


def unpack(tiles, wtiles):
    lat_wins = 2
    return pl.pallas_call(
        unpack_kernel,
        grid=(2,),
        out_shape=[
            jax.ShapeDtypeStruct((2, 2, lat_wins, HEADS, WIN * WIN), F32),
            jax.ShapeDtypeStruct((2, C, 3 * C), F32),
            jax.ShapeDtypeStruct((2, C, C), F32),
        ],
        in_specs=[
            pl.BlockSpec((ZS, 1, CHUNK, 16, 128), lambda l: (0, l, 0, 0, 0)),
            pl.BlockSpec((72, 16, 128), lambda l: (l, 0, 0)),
        ],
        out_specs=[
            pl.BlockSpec((1, 2, lat_wins, HEADS, WIN * WIN), lambda l: (l, 0, 0, 0, 0)),
            pl.BlockSpec((1, C, 3 * C), lambda l: (l, 0, 0)),
            pl.BlockSpec((1, C, C), lambda l: (l, 0, 0)),
        ],
        compiler_params=pltpu.CompilerParams(vmem_limit_bytes=VMEM_LIMIT),
    )(tiles, wtiles)


def shards(tokens, cotangent, w_qkv, w_proj, w_in, w_out, earth_bias):
    load, own, send, recv = (jnp.asarray(m, BF16) for m in _matrices())
    matrices = {"loadt": load.T, "own2": own.T, "send2": recv.T, "recv2": send.T}
    params = [w_qkv, w_proj, w_in, w_out]
    flat = (48, 12, C)
    main, rest = [((WIN * 8, 128), F32)] * 2
    main24, rest24 = [((WIN * 24, 128), F32)] * 2
    tok = ((TOK, C), BF16)
    qkv = ((TOK, 3 * C), BF16)
    qkvt = ((4, 3 * C, WIN), BF16)
    prob = ((24, WIN, WIN), F32)
    mixedt = ((4, C, WIN), BF16)
    slope = ((TOK, FF), F32)
    tiles = ((256, 16, 128), BF16)
    wtiles = ((72, 16, 128), BF16)
    back_scratch = [tok, tok, ((3 * C, WIN), BF16), tok, ((C, FF), F32)]
    kept_state = [tok, tok, qkv, qkvt, prob, mixedt, tok, slope]

    *state, kept, sent = compute_call(
        forward_kernel,
        [tokens.reshape(flat), cotangent.reshape(flat), load, own, send]
        + [(p, 0) for p in params]
        + [(earth_bias, 0)],
        kept_state + [((2, TOK, C), BF16), ((2, SEND, C), BF16)],
        [((768, C), BF16), tok, main, rest],
    )
    arrived = exchange(sent, -1, 0)
    kept, sent, tiles1, w1 = compute_call(
        middle_kernel,
        [kept, arrived, recv, matrices["send2"], matrices["own2"]]
        + [(p, 1) for p in params]
        + [(earth_bias, 1)],
        [tok, ((SEND, C), BF16), tiles, wtiles],
        [tok, qkv, qkvt, prob, mixedt, tok] + back_scratch + [main, rest, main24, rest24],
    )
    arrived = exchange(sent[None], 1, 1)[0]
    grid, tiles0, w0 = compute_call(
        backward_kernel,
        [kept, arrived, matrices["recv2"], matrices["loadt"]] + state + [(p, 0) for p in params],
        [(flat, BF16), tiles, wtiles],
        back_scratch + [main24, rest24],
    )
    total, wtotal = reduce_all(tiles0, tiles1, w0, w1)
    bias_total, qkv_total, proj_total = unpack(total, wtotal)
    return grid.reshape(tokens.shape), qkv_total, proj_total, bias_total


def solution(mesh):
    return jax.shard_map(
        shards,
        mesh=mesh,
        in_specs=(
            P(None, "lat", "lon", None),
            P(None, "lat", "lon", None),
            P(),
            P(),
            P(),
            P(),
            P(None, None, "lat", None, None),
        ),
        out_specs=(P(None, "lat", "lon", None), P(), P(), P(None, None, "lat", None, None)),
        check_vma=False,
    )
```

profile of v0, /device:TPU:8, one launch (start us, length us, event | category | flops | bytes accessed | tf_op | source)
XLA Modules:
  0.0 198.0 jit_solution(2694503800507640437)
XLA Ops:
  0.6 0.0 copy-start
  0.6 1.9 copy.15
  2.5 1.8 copy.16
  4.3 2.2 %copy.17.w_out = bf16[2,768,192]{2,1,0:T(8,128)(2,1)} copy(bf16[2,768,192]{1,2,0:T(8,128)(2,1)} %param.16) | data formatting | bytes 1179648 | tf_op args[5]
  6.5 0.0 copy-done
  6.5 1.8 copy.18.bias_ref
  8.3 22.9 %shard_map.138 = (bf16[576,192]{1,0:T(8,128)(2,1)}, bf16[576,192]{1,0:T(8,128)(2,1)}, bf16[576,576]{1,0:T(8,128)(2,1)}, bf16[4,576,144]{2,1,0:T(8,128)(2,1)}, f3...) custom-call(bf16[48,12,192]{2,1,0:T(8,128)(2,1)} %bitcast.5, ...), custom_call_target="tpu_custom_call" | custom-call | tf_op jit(solution)/shard_map/pallas_call | solution.py:348
  31.2 15.6 %shard_map.139.arrived_ref = bf16[2,384,192]{2,1,0:T(8,128)(2,1)} custom-call(bf16[2,384,192]{2,1,0:T(8,128)(2,1)} %get-tuple-element.27.send_ref), custom_call_target="tpu_custom_call" | custom-call | tf_op jit(solution)/shard_map/pallas_call | solution.py:391
  46.8 32.9 %shard_map.140 = (bf16[576,192]{1,0:T(8,128)(2,1)}, bf16[384,192]{1,0:T(8,128)(2,1)}, bf16[256,16,128]{2,1,0:T(8,128)(2,1)}, bf16[72,16,128]{2,1,0:T(8,128)(2,1)}) custom-call(bf16[2,576,192]{2,1,0:T(8,128)(2,1)} %get-tuple-element.26.kept_ref, bf16[2,384,192]{2,1,0:T(8,128)(2,1)} %shard_map.139.arrived_ref, bf16[576,384]{1,0:T(8,128)(2,1)} %constant.11.clone.recv_ref, ...), custom_call_target="tpu_custom_call" | custom-call | tf_op jit(solution)/shard_map/pallas_call | solution.py:348
  79.7 13.2 %shard_map.141 = bf16[1,384,192]{2,1,0:T(8,128)(2,1)} custom-call(bf16[1,384,192]{2,1,0:T(8,128)(2,1)} %bitcast.9), custom_call_target="tpu_custom_call" | custom-call | tf_op jit(solution)/shard_map/pallas_call | solution.py:391
  92.9 18.2 %shard_map.142 = (bf16[48,12,192]{2,1,0:T(8,128)(2,1)}, bf16[256,16,128]{2,1,0:T(8,128)(2,1)}, bf16[72,16,128]{2,1,0:T(8,128)(2,1)}) custom-call(bf16[576,192]{1,0:T(8,128)(2,1)} %get-tuple-element.28.kept_ref, bf16[384,192]{1,0:T(8,128)(2,1)} %bitcast.7, bf16[576,384]{1,0:T(8,128)(2,1)} %constant.17.recv2_ref, bf16[768,576]{1,0:T(8,128)(2,1)} %constant.18.loadt_ref, ...), custom_call_target="tpu_custom_call" | custom-call | tf_op jit(solution)/shard_map/pallas_call | solution.py:348
  111.1 1.9 copy.22
  113.0 74.3 %shard_map.143 = (bf16[8,2,32,16,128]{4,3,2,1,0:T(8,128)(2,1)}, bf16[144,16,128]{2,1,0:T(8,128)(2,1)}) custom-call(bf16[256,16,128]{2,1,0:T(8,128)(2,1)} %get-tuple-element.39.tiles0, bf16[256,16,128]{2,1,0:T(8,128)(2,1)} %get-tuple-element.40.tiles1, bf16[72,16,128]{2,1,0:T(8,128)(2,1)} %get-tuple-element.41.w0, bf16[72,16,128]{2,1,0:T(8,128)(2,1)} %get-tuple-element.42.w1), custom_call_target="tpu_custom_call" | custom-call | tf_op jit(solution)/shard_map/pallas_call | solution.py:578
  187.3 4.1 %shard_map.144 = (f32[2,2,2,6,20736]{4,3,2,1,0:T(8,128)}, f32[2,192,576]{2,1,0:T(8,128)}, f32[2,192,192]{2,1,0:T(8,128)}) custom-call(bf16[8,2,32,16,128]{4,3,2,1,0:T(8,128)(2,1)} %get-tuple-element.43.tiles_ref, bf16[144,16,128]{2,1,0:T(8,128)(2,1)} %get-tuple-element.44.wtiles_ref), custom_call_target="tpu_custom_call" | custom-call | tf_op jit(solution)/shard_map/pallas_call | solution.py:612
  191.5 6.5 %copy.23 = f32[2,2,2,6,20736]{4,2,3,1,0:T(2,128)} copy(f32[2,2,2,6,20736]{4,3,2,1,0:T(8,128)} %get-tuple-element.51) | data formatting | bytes 7962624
Async XLA Ops:
  0.6 5.9 %copy-start = (bf16[2,2,2,6,20736]{4,2,3,1,0:T(2,128)(2,1)S(1)}, bf16[2,2,2,6,20736]{4,2,3,1,0:T(2,128)(2,1)}, u32[]{:S(2)}) copy-start(bf16[2,2,2,6,20736]{4,2,3,1,0:T(2,128)(2,1)} %param.17) | copy-start | bytes 5971972
where the time goes:
time: 199 us; the launch traced here: 198 us
  Pallas kernels  181 us (91%)
  local copies, waits for them, and re-layouts  16.1 us (8%)
    pallas_call x1, Pallas kernels, reduce_all(): pl.pallas_call(reduce_kernel, out_shape=[jax.ShapeDtypeStruct((ZS,) + rin...  74.3 us
    pallas_call x3, Pallas kernels, compute_call(): pl.pallas_call(kernel, out_shape=[jax.ShapeDtypeStruct(shape, kind) for s...  74 us
    pallas_call x2, Pallas kernels, exchange(): pl.pallas_call(functools.partial(exchange_kernel, sign), out_shape=jax.Sh...  28.7 us
    unnamed x8, local copies, waits for them, and re-layouts  16.1 us
    pallas_call x1, Pallas kernels, unpack(): pl.pallas_call(unpack_kernel, grid=(2,), out_shape=[jax.ShapeDtypeStruct(...  4.15 us

commit v1 on v0

v1 whole, which is shorter than its diff:
```python
import functools

import jax
import jax.numpy as jnp
import numpy as np
from jax import lax
from jax.experimental import pallas as pl
from jax.experimental.pallas import tpu as pltpu
from jax.sharding import PartitionSpec as P

F32 = jnp.float32
BF16 = jnp.bfloat16
C = 192
HEADS = 6
HD = 32
FF = 768
WIN = 144
TOK = 576
EPSILON = 1e-05
SCALE = HD ** (-0.5)
MESH = pl.DeviceIdType.MESH
E0, S0, D0, SEND = 0, 224, 304, 384
VMEM_LIMIT = 48 * 1024 * 1024
ZS = 8
PAIRS = 12
FLAT = 3888
ROWS = 4096


def _plain_index(level, row, col):
    window = (level // 2) * 2 + row // 6
    return window * WIN + (level % 2) * 72 + (row % 6) * 12 + col


def _matrices():
    load = np.zeros((TOK, 768), np.float32)
    own = np.zeros((TOK, TOK), np.float32)
    send = np.zeros((SEND, TOK), np.float32)
    recv = np.zeros((TOK, SEND), np.float32)
    for level in range(4):
        for row in range(12):
            for col in range(12):
                here = _plain_index(level, row, col)
                load[here, (level * 12 + row) * 16 + col] = 1
                target_row, target_col = row - 3, col - 6
                target = _plain_index((level - 1) % 4, target_row % 12, target_col % 12)
                if target_row >= 0 and target_col >= 0:
                    own[target, here] = 1
                    continue
                if target_row >= 0:
                    slot = E0 + (level * 9 + row - 3) * 6 + col
                elif target_col >= 0:
                    slot = S0 + (level * 3 + row) * 6 + col - 6
                else:
                    slot = D0 + (level * 3 + row) * 6 + col
                send[slot, here] = 1
                recv[target, slot] = 1
    return load, own, send, recv


def nn(a, b):
    return jnp.dot(a, b, preferred_element_type=F32)


def nt(a, b):
    return lax.dot_general(a, b, (((1,), (1,)), ((), ())), preferred_element_type=F32)


def eye(n):
    rows = lax.broadcasted_iota(jnp.int32, (n, n), 0)
    cols = lax.broadcasted_iota(jnp.int32, (n, n), 1)
    return jnp.where(rows == cols, 1.0, 0.0).astype(BF16)


def flip(a, n):
    return nt(eye(n), a).astype(BF16)


def normalize(x):
    center = jnp.mean(x, axis=-1, keepdims=True)
    offset = x - center
    spread = jnp.mean(offset * offset, axis=-1, keepdims=True)
    inverse = lax.rsqrt(spread + EPSILON)
    return offset * inverse, inverse


def norm_back(x, upstream):
    normed, inverse = normalize(x)
    first = jnp.mean(upstream, axis=-1, keepdims=True)
    second = jnp.mean(upstream * normed, axis=-1, keepdims=True)
    return inverse * (upstream - first - normed * second)


def cumulative(x):
    return 0.5 * (1.0 + lax.erf(x * 0.7071067811865476))


def density(x):
    return 0.3989422804014327 * jnp.exp(-0.5 * x * x)


def rows_of(window):
    return pl.ds(pl.multiple_of(window * WIN, WIN), WIN)


def spread_bias(bias_ref, window, main, rest):
    def step(group, carry):
        block = bias_ref[
            0, window // 2, window % 2, :, pl.ds(pl.multiple_of(group * 1152, 128), 1152)
        ].astype(F32)
        for r in range(8):
            at = pl.ds(pl.multiple_of(group * 64, 64) + 8 * r, 6)
            main[at, :] = block[:, WIN * r : WIN * r + 128]
            rest[at, 0:16] = block[:, WIN * r + 128 : WIN * r + WIN]
        return carry

    lax.fori_loop(0, 18, step, 0)


def head_bias(main, rest, head):
    left = main[pl.ds(head, WIN, stride=8), :]
    right = rest[pl.ds(head, WIN, stride=8), :]
    return jnp.concatenate([left, right[:, :16]], axis=1)


def pack_bias(main, rest, out_ref):
    def flat(first):
        parts = []
        for r in range(8):
            at = pl.ds(pl.multiple_of(first * 192, 8) + 24 * r, 24)
            parts += [main[at, :], rest[at, :][:, :16]]
        return jnp.concatenate(parts, axis=1)

    def step(group, carry):
        top = flat(group)
        bottom = flat(group + 9)
        for third in range(3):
            both = jnp.concatenate(
                [top[8 * third : 8 * third + 8], bottom[8 * third : 8 * third + 8]], axis=0
            ).astype(BF16)
            for j in range(9):
                out_ref[third * 81 + group * 9 + j] = both[:, 128 * j : 128 * j + 128]
        return carry

    lax.fori_loop(0, 9, step, 0)
    out_ref[243:256] = jnp.zeros((13, 16, 128), BF16)


def pack_weights(wgrad, out_ref):
    for i in range(12):
        block = wgrad[16 * i : 16 * i + 16, :].astype(BF16)
        for j in range(6):
            out_ref[6 * i + j] = block[:, 128 * j : 128 * j + 128]
    out_ref[72:80] = jnp.zeros((8, 16, 128), BF16)


def attention_forward(window, qkv_ref, qkvt_ref, prob_ref, mixedt_ref, mixed_ref, biases, mask):
    bias_ref, main, rest = biases
    spread_bias(bias_ref, window, main, rest)
    qkv = qkv_ref[rows_of(window), :]
    qkvt_ref[window] = flip(qkv, 3 * C)
    for head in range(HEADS):
        lo = head * HD
        keys = qkvt_ref[window, C + lo : C + lo + HD, :]
        values = qkvt_ref[window, 2 * C + lo : 2 * C + lo + HD, :]
        scores = nn(qkv[:, lo : lo + HD], keys) * SCALE + head_bias(main, rest, head)
        weights = jnp.exp(scores)
        if mask is not None:
            weights = weights * mask
        probs = weights / jnp.sum(weights, axis=-1, keepdims=True)
        probs = probs.astype(BF16)
        prob_ref[window * HEADS + head] = probs
        mixedt_ref[window, lo : lo + HD, :] = nt(values, probs).astype(BF16)
    mixed_ref[rows_of(window), :] = flip(mixedt_ref[window], WIN)


def attention_backward(
    window, source_ref, qkvt_ref, prob_ref, mixedt_ref, mgrad_ref, grad_ref,
    w_qkv, w_proj, gradt, sgrad_ref, wgrad, table,
):
    mgrad = mgrad_ref[rows_of(window), :]
    wgrad[:, 3 * C :] += nn(mixedt_ref[window], mgrad)
    grad = grad_ref[rows_of(window), :]
    gt = nt(w_proj, mgrad).astype(BF16)
    for head in range(HEADS):
        lo = head * HD
        queries = qkvt_ref[window, lo : lo + HD, :]
        keys = qkvt_ref[window, C + lo : C + lo + HD, :]
        values = qkvt_ref[window, 2 * C + lo : 2 * C + lo + HD, :]
        probs = prob_ref[window * HEADS + head]
        pgrad = nn(grad[:, lo : lo + HD], values)
        vgrad = nn(gt[lo : lo + HD, :], probs)
        probs = probs.astype(F32)
        delta = jnp.sum(pgrad * probs, axis=-1, keepdims=True)
        sgrad = probs * (pgrad - delta)
        at = pl.ds(window * HEADS + head, WIN, stride=24)
        table[0][at, :] = sgrad[:, :128]
        table[1][at, :] = jnp.concatenate([sgrad[:, 128:], jnp.zeros((WIN, 112), F32)], axis=1)
        sround = sgrad.astype(BF16)
        gradt[lo : lo + HD, :] = (nt(keys, sround) * SCALE).astype(BF16)
        gradt[C + lo : C + lo + HD, :] = (nn(queries, sround) * SCALE).astype(BF16)
        gradt[2 * C + lo : 2 * C + lo + HD, :] = vgrad.astype(BF16)
    all_grad = gradt[...]
    sourcet = flip(source_ref[rows_of(window), :], C)
    wgrad[:, : 3 * C] += nt(sourcet, all_grad)
    sgradt = nn(w_qkv, all_grad).astype(BF16)
    sgrad_ref[rows_of(window), :] = flip(sgradt, WIN)


def mlp_back(middle, upstream, slope, w_in, w_outt):
    act_grad = nn(upstream, w_outt)
    pre_grad = (slope * act_grad).astype(BF16)
    ngrad = nt(pre_grad, w_in)
    return (upstream.astype(F32) + norm_back(middle.astype(F32), ngrad)).astype(BF16)


def region_mask(window):
    last_lat = lax.axis_index("lat") == lax.axis_size("lat") - 1

    def region(tokens):
        level = tokens // 72
        row = tokens // 12 % 6
        upper = jnp.where(window // 2 == 1, level, 0)
        lower = jnp.where(jnp.logical_and(last_lat, window % 2 == 1), row // 3, 0)
        return upper * 2 + lower

    queries = region(lax.broadcasted_iota(jnp.int32, (WIN, WIN), 0))
    keys = region(lax.broadcasted_iota(jnp.int32, (WIN, WIN), 1))
    return jnp.where(queries == keys, 1.0, 0.0)


def place():
    lat, lon = lax.axis_index("lat"), lax.axis_index("lon")
    return lat, lon, lax.rem(lon, ZS), lon // ZS


def neighbour(lat_steps, lon_steps):
    lats, lons = lax.axis_size("lat"), lax.axis_size("lon")
    lat, lon, _, _ = place()
    return lax.rem(lat + lat_steps + lats, lats), lax.rem(lon + lon_steps + lons, lons)


def remote(src, dst, send, recv, device):
    return pltpu.make_async_remote_copy(
        src_ref=src, dst_ref=dst, send_sem=send, recv_sem=recv, device_id=device, device_id_type=MESH
    )


def wait_all(copies):
    for copy in copies:
        copy.wait()


def greet():
    barrier = pltpu.get_barrier_semaphore()
    for k in range(1, 16):
        for device in (neighbour(k, 0), neighbour(0, k)):
            pl.semaphore_signal(barrier, inc=1, device_id=device, device_id_type=MESH)
    pl.semaphore_wait(barrier, 30)


def exchange_kernel(sign, send_ref, out_ref, send_sems, recv_sems):
    barrier = pltpu.get_barrier_semaphore()
    steps = [(0, sign, E0, S0), (sign, 0, S0, D0), (sign, sign, D0, SEND)]
    for lat, lon, _, _ in steps:
        pl.semaphore_signal(barrier, inc=1, device_id=neighbour(-lat, -lon), device_id_type=MESH)
    pl.semaphore_wait(barrier, 3)
    copies = []
    for i, (lat, lon, start, stop) in enumerate(steps):
        piece = pl.ds(start, stop - start)
        copy = pltpu.make_async_remote_copy(
            src_ref=send_ref.at[:, piece],
            dst_ref=out_ref.at[:, piece],
            send_sem=send_sems.at[i],
            recv_sem=recv_sems.at[i],
            device_id=neighbour(lat, lon),
            device_id_type=MESH,
        )
        copy.start()
        copies.append(copy)
    for copy in copies:
        copy.wait()


def exchange(sent, sign, collective_id):
    return pl.pallas_call(
        functools.partial(exchange_kernel, sign),
        out_shape=jax.ShapeDtypeStruct(sent.shape, BF16),
        in_specs=[pl.BlockSpec(memory_space=pltpu.VMEM)],
        out_specs=pl.BlockSpec(memory_space=pltpu.VMEM),
        scratch_shapes=[pltpu.SemaphoreType.DMA((3,)), pltpu.SemaphoreType.DMA((3,))],
        compiler_params=pltpu.CompilerParams(collective_id=collective_id, has_side_effects=True),
    )(sent)


class Ring:
    def __init__(self, rows, own, out, base, bufs, sems):
        self.rows, self.own, self.out, self.base = rows, own, out, base
        self.right_in, self.left_in, self.right_sum, self.left_sum = bufs
        self.sems = sems
        lat, lon, self.z, y = place()
        self.right = (lat, y * ZS + lax.rem(self.z + 1, ZS))
        self.left = (lat, y * ZS + lax.rem(self.z + ZS - 1, ZS))
        self.sums, self.gathers = [], []

    def chunk(self, steps):
        return pl.multiple_of(lax.rem(self.z + steps + 2 * ZS, ZS) * self.rows, self.rows)

    def send(self, kind, step, src, dst, device):
        copy = remote(src, dst, self.sems.at[kind, step], self.sems.at[kind + 1, step], device)
        copy.start()
        return copy

    def reduce(self, step):
        if step:
            for copy in self.sums[-1]:
                copy.wait_recv()
        now = []
        value = self.own(self.chunk(4 - step))
        if step:
            value = (value.astype(F32) + self.right_in[step - 1].astype(F32)).astype(BF16)
        self.right_sum[step] = value
        now.append(self.send(0, step, self.right_sum.at[step], self.right_in.at[step], self.right))
        if step < 3:
            value = self.own(self.chunk(step - 3))
            if step:
                value = (value.astype(F32) + self.left_in[step - 1].astype(F32)).astype(BF16)
            self.left_sum[step] = value
            now.append(self.send(2, step, self.left_sum.at[step], self.left_in.at[step], self.left))
        self.sums.append(now)

    def total(self):
        self.sums[3][0].wait_recv()
        return self.own(self.chunk(0)).astype(F32) + self.right_in[3].astype(F32) + self.left_in[2].astype(F32)

    def piece(self, steps):
        return self.out.at[pl.ds(pl.multiple_of(self.base + self.chunk(steps), self.rows), self.rows)]

    def gather(self, step):
        came = []
        if step:
            for copy in self.gathers[-1]:
                copy.wait_recv()
            came.append((step, self.piece(-step)))
            if step < 4:
                came.append((step + 4, self.piece(step)))
        if step < 4:
            now = [self.send(4, step, self.piece(-step), self.piece(-step), self.right)]
            if step < 3:
                now.append(self.send(6, step, self.piece(step), self.piece(step), self.left))
            self.gathers.append(now)
        return came

    def finish(self):
        for now in self.sums + self.gathers:
            for copy in now:
                copy.wait_send()


def sum_tiles(tiles, out, bufs, sems, y_sems):
    lat, lon, z, y = place()
    partner = (lat, (1 - y) * ZS + z)
    bufs_a, mine, other, bufs_b, half, half_in = bufs
    a = Ring(256, lambda at: tiles[pl.ds(at, 256)], out, 0, bufs_a, sems.at[0])
    base = 2048 + y * 1024
    b = Ring(128, lambda at: half[pl.ds(at, 128)], out, base, bufs_b, sems.at[1])
    away = pl.ds(pl.multiple_of(2048 + (1 - y) * 1024, 1024), 1024)
    here = pl.ds(pl.multiple_of(2048 + y * 1024, 1024), 1024)
    cross = remote(tiles.at[away], half_in, y_sems.at[0, 0], y_sems.at[1, 0], partner)
    cross.start()
    a.reduce(0)
    yield
    a.reduce(1)
    yield
    cross.wait_recv()
    half[...] = (tiles[here].astype(F32) + half_in[...].astype(F32)).astype(BF16)
    b.reduce(0)
    a.reduce(2)
    yield
    b.reduce(1)
    a.reduce(3)
    yield
    b.reduce(2)
    mine[...] = a.total().astype(BF16)
    swap = remote(mine, other, y_sems.at[0, 1], y_sems.at[1, 1], partner)
    swap.start()
    yield
    b.reduce(3)
    swap.wait_recv()
    a.piece(0)[...] = (mine[...].astype(F32) + other[...].astype(F32)).astype(BF16)
    a.gather(0)
    yield
    b.piece(0)[...] = b.total().astype(BF16)
    b.gather(0)
    shared = []

    def share(pieces):
        for slot, piece in pieces:
            copy = remote(piece, piece, y_sems.at[0, 2 + slot], y_sems.at[1, 2 + slot], partner)
            copy.start()
            shared.append(copy)

    share([(0, b.piece(0))])
    a.gather(1)
    yield
    share(b.gather(1))
    a.gather(2)
    yield
    share(b.gather(2))
    a.gather(3)
    yield
    share(b.gather(3))
    a.gather(4)
    yield
    share(b.gather(4))
    wait_all(shared)
    cross.wait_send()
    swap.wait_send()
    a.finish()
    b.finish()


def sum_weights(w, out, part, mid, owned, done, sems, first):
    lat, lon, _, _ = place()
    peers = range(1, 16)
    scatter = []
    for k in peers:
        to = neighbour(k, 0)
        copy = remote(w.at[pl.ds(to[0] * 5, 5)], part.at[k], sems.at[0, k], sems.at[1, k], to)
        copy.start()
        scatter.append(copy)
    yield
    total = w[pl.ds(lat * 5, 5)].astype(F32)
    for k, copy in enumerate(scatter, 1):
        copy.wait_recv()
        total = total + part[k].astype(F32)
    mid[...] = total.astype(BF16)

    def owner(index):
        return jnp.logical_and(index >= first, index < first + 5)

    def to_owner(k, device):
        tile = jnp.clip(device[1] - first, 0, 4)
        return remote(mid.at[tile], owned.at[k], sems.at[2, k], sems.at[3, k], device)

    def from_owner(k, tile, device):
        tile = jnp.clip(tile, 0, 4)
        return remote(done.at[tile], done.at[tile], sems.at[4, k], sems.at[5, k], device)

    for k in peers:
        to = neighbour(0, k)

        @pl.when(owner(to[1]))
        def _():
            to_owner(k, to).start()

    yield

    @pl.when(owner(lon))
    def _():
        mine = jnp.clip(lon - first, 0, 4)
        value = mid[mine].astype(F32)
        for k in peers:
            to_owner(k, (lat, lon)).wait_recv()
            value = value + owned[k].astype(F32)
        done[mine] = value.astype(BF16)
        for k in peers:
            from_owner(k, lon - first, neighbour(0, k)).start()

    yield
    for k in peers:
        source = neighbour(0, -k)

        @pl.when(owner(source[1]))
        def _():
            from_owner(k, source[1] - first, source).wait_recv()

    out[pl.ds(lat * 5, 5)] = done[...]
    spread = []
    for k in peers:
        piece = out.at[pl.ds(lat * 5, 5)]
        copy = remote(piece, piece, sems.at[6, k], sems.at[7, k], neighbour(k, 0))
        copy.start()
        spread.append(copy)
    yield
    wait_all(spread)
    for copy in scatter:
        copy.wait_send()
    for k in peers:
        to = neighbour(0, k)

        @pl.when(owner(to[1]))
        def _():
            to_owner(k, to).wait_send()

    @pl.when(owner(lon))
    def _():
        for k in peers:
            from_owner(k, lon - first, neighbour(0, k)).wait_send()


def advance(*streams):
    for stream in streams:
        next(stream, None)


def drain(*streams):
    live = list(streams)
    while live:
        live = [stream for stream in live if next(stream, live) is not live]


def attention_block(x, source, qkv, qkvt, prob, mixedt, mixed, w_qkv, w_proj, w_in, biases, masked):
    source[...] = normalize(x)[0].astype(BF16)
    qkv[...] = nn(source[...], w_qkv[0]).astype(BF16)

    def step(window, carry):
        attention_forward(
            window, qkv, qkvt, prob, mixedt, mixed, biases, region_mask(window) if masked else None
        )
        return carry

    lax.fori_loop(0, 4, step, 0)
    attended = nn(mixed[...], w_proj[0]).astype(BF16)
    middle = (x + attended.astype(F32)).astype(BF16)
    pre = nn(normalize(middle.astype(F32))[0].astype(BF16), w_in[0])
    phi = cumulative(pre)
    return middle, pre, phi, phi + pre * density(pre)


def load_grid(grid_ref, pad, matrix):
    for i in range(48):
        pad[16 * i : 16 * i + 12, :] = grid_ref[i]
    return nn(matrix, pad[...])


def forward_kernel(
    tok_ref, cot_ref, load_ref, own_ref, send_ref, w_qkv, w_proj, w_in, w_outt, bias_ref,
    x_out, source, qkvt, prob, mixedt, mid_out, slope_out, kept, sent,
    qkv, mixed, main, rest, pad,
):
    pad[...] = jnp.zeros_like(pad)
    cot = load_grid(cot_ref, pad, load_ref[...]).astype(BF16)
    sent[1] = nn(send_ref[...], cot).astype(BF16)
    kept[1] = nn(own_ref[...], cot).astype(BF16)
    x0 = load_grid(tok_ref, pad, load_ref[...])
    x_out[...] = x0.astype(BF16)
    middle, pre, phi, slope = attention_block(
        x0, source, qkv, qkvt, prob, mixedt, mixed, w_qkv, w_proj, w_in, (bias_ref, main, rest), False
    )
    mid_out[...] = middle
    slope_out[...] = slope.astype(BF16)
    x1 = (middle.astype(F32) + nt((pre * phi).astype(BF16), w_outt[0])).astype(BF16)
    sent[0] = nn(send_ref[...], x1).astype(BF16)
    kept[0] = nn(own_ref[...], x1).astype(BF16)


def middle_kernel(
    kept, arrived, recv_ref, ownt_ref, recvt_ref, w_qkv, w_proj, w_in, w_outt, bias_ref,
    kept_out, sent, tiles, wtiles,
    source, qkv, qkvt, prob, mixedt, mixed, mgrad, grad, gradt, sgrad, wgrad, main24, rest24, main, rest,
):
    x1 = kept[0].astype(F32) + nn(recv_ref[...], arrived[0])
    middle, _, _, slope = attention_block(
        x1, source, qkv, qkvt, prob, mixedt, mixed, w_qkv, w_proj, w_in, (bias_ref, main, rest), True
    )
    cot = (kept[1].astype(F32) + nn(recv_ref[...], arrived[1])).astype(BF16)
    mgrad[...] = mlp_back(middle, cot, slope, w_in[0], w_outt[0])
    grad[...] = nt(mgrad[...], w_proj[0]).astype(BF16)
    wgrad[...] = jnp.zeros_like(wgrad)

    def back(window, carry):
        attention_backward(
            window, source, qkvt, prob, mixedt, mgrad, grad, w_qkv[0], w_proj[0], gradt, sgrad, wgrad, (main24, rest24)
        )
        return carry

    lax.fori_loop(0, 4, back, 0)
    result = (mgrad[...].astype(F32) + norm_back(x1, sgrad[...].astype(F32))).astype(BF16)
    sent[0] = nn(recvt_ref[...], result).astype(BF16)
    kept_out[...] = nn(ownt_ref[...], result).astype(BF16)
    pack_bias(main24, rest24, tiles)
    pack_weights(wgrad, wtiles)


def backward_kernel(
    kept, arrived, sendt_ref, loadt_ref, x_ref, source, qkvt, prob, mixedt, mid, slope,
    w_qkv, w_proj, w_in, w_outt,
    grid_out, tiles, wtiles,
    mgrad, grad, gradt, sgrad, wgrad, main24, rest24,
):
    upstream = (kept[...].astype(F32) + nn(sendt_ref[...], arrived[0])).astype(BF16)
    mgrad[...] = mlp_back(mid[...], upstream, slope[...].astype(F32), w_in[0], w_outt[0])
    grad[...] = nt(mgrad[...], w_proj[0]).astype(BF16)
    wgrad[...] = jnp.zeros_like(wgrad)

    def back(window, carry):
        attention_backward(
            window, source, qkvt, prob, mixedt, mgrad, grad, w_qkv[0], w_proj[0], gradt, sgrad, wgrad, (main24, rest24)
        )
        return carry

    lax.fori_loop(0, 4, back, 0)
    result = (mgrad[...].astype(F32) + norm_back(x_ref[...].astype(F32), sgrad[...].astype(F32))).astype(BF16)
    placed = nn(loadt_ref[...], result).astype(BF16)
    for i in range(48):
        grid_out[i] = placed[16 * i : 16 * i + 12, :]
    pack_bias(main24, rest24, tiles)
    pack_weights(wgrad, wtiles)


def compute_call(kernel, operands, outs, scratch):
    specs, arrays = [], []
    once = pl.Buffered(1)
    for operand in operands:
        array, layer = operand if isinstance(operand, tuple) else (operand, None)
        arrays.append(array)
        shape = array.shape if layer is None else (1,) + array.shape[1:]
        index = (0 if layer is None else layer,) + (0,) * (array.ndim - 1)
        specs.append(pl.BlockSpec(shape, functools.partial(lambda at, _: at, index), pipeline_mode=once))
    return pl.pallas_call(
        kernel,
        out_shape=[jax.ShapeDtypeStruct(shape, kind) for shape, kind in outs],
        grid=(1,),
        in_specs=specs,
        out_specs=[
            pl.BlockSpec(shape, functools.partial(lambda at, _: at, (0,) * len(shape)), pipeline_mode=once)
            for shape, kind in outs
        ],
        scratch_shapes=[pltpu.VMEM(shape, kind) for shape, kind in scratch],
        compiler_params=pltpu.CompilerParams(vmem_limit_bytes=VMEM_LIMIT),
    )(*arrays)


def sum_kernel(
    tiles0, tiles1, wtiles0, wtiles1, bias_out, w_out,
    a_right_in, a_left_in, a_right_sum, a_left_sum, mine, other,
    b_right_in, b_left_in, b_right_sum, b_left_sum, half, half_in, ring_sems, y_sems,
    wpart, wmid, wowned, wdone, w_sems,
):
    greet()
    streams = []
    for layer, (tiles, wtiles) in enumerate(((tiles0, wtiles0), (tiles1, wtiles1))):
        bufs_a = [ref.at[layer] for ref in (a_right_in, a_left_in, a_right_sum, a_left_sum)]
        bufs_b = [ref.at[layer] for ref in (b_right_in, b_left_in, b_right_sum, b_left_sum)]
        bufs = (bufs_a, mine.at[layer], other.at[layer], bufs_b, half.at[layer], half_in.at[layer])
        streams.append(sum_tiles(tiles, bias_out.at[layer], bufs, ring_sems.at[layer], y_sems.at[layer]))
        streams.append(
            sum_weights(
                wtiles, w_out.at[layer], wpart.at[layer], wmid.at[layer], wowned.at[layer],
                wdone.at[layer], w_sems.at[layer], 8 * layer,
            )
        )
    drain(*streams)


def sum_all(tiles0, tiles1, wtiles0, wtiles1):
    vmem, dma = pltpu.VMEM, pltpu.SemaphoreType.DMA

    def ring(rows):
        return [vmem((2, n, rows, 128), BF16) for n in (4, 3, 4, 3)]

    return pl.pallas_call(
        sum_kernel,
        out_shape=[
            jax.ShapeDtypeStruct((2, ROWS, 128), BF16),
            jax.ShapeDtypeStruct((2, 80, 16, 128), BF16),
        ],
        in_specs=[pl.BlockSpec(memory_space=vmem)] * 4,
        out_specs=[pl.BlockSpec(memory_space=vmem)] * 2,
        scratch_shapes=[
            *ring(256),
            vmem((2, 256, 128), BF16),
            vmem((2, 256, 128), BF16),
            *ring(128),
            vmem((2, 1024, 128), BF16),
            vmem((2, 1024, 128), BF16),
            dma((2, 2, 8, 4)),
            dma((2, 2, 10)),
            vmem((2, 16, 5, 16, 128), BF16),
            vmem((2, 5, 16, 128), BF16),
            vmem((2, 16, 16, 128), BF16),
            vmem((2, 5, 16, 128), BF16),
            dma((2, 8, 16)),
        ],
        compiler_params=pltpu.CompilerParams(
            collective_id=2, has_side_effects=True, vmem_limit_bytes=VMEM_LIMIT
        ),
    )(tiles0, tiles1, wtiles0, wtiles1)


def unpack_kernel(tiles_ref, wtiles_ref, bias_out, qkv_out, proj_out):
    for j in range(81):
        rows = [tiles_ref[0, 16 * (third * 81 + j) : 16 * (third * 81 + j) + 16, :].astype(F32) for third in range(3)]
        for half in range(2):
            lanes = slice(half * 10368 + 128 * j, half * 10368 + 128 * j + 128)
            full = jnp.concatenate([part[8 * half : 8 * half + 8] for part in rows], axis=0)
            for window in range(4):
                bias_out[0, window // 2, window % 2, :, lanes] = full[6 * window : 6 * window + 6]
    for i in range(12):
        row = jnp.concatenate([wtiles_ref[0, 6 * i + j].astype(F32) for j in range(6)], axis=1)
        qkv_out[0, 16 * i : 16 * i + 16, :] = row[:, : 3 * C]
        proj_out[0, 16 * i : 16 * i + 16, :] = row[:, 3 * C :]


def unpack(tiles, wtiles):
    return pl.pallas_call(
        unpack_kernel,
        grid=(2,),
        out_shape=[
            jax.ShapeDtypeStruct((2, 2, 2, HEADS, WIN * WIN), F32),
            jax.ShapeDtypeStruct((2, C, 3 * C), F32),
            jax.ShapeDtypeStruct((2, C, C), F32),
        ],
        in_specs=[
            pl.BlockSpec((1, ROWS, 128), lambda l: (l, 0, 0)),
            pl.BlockSpec((1, 80, 16, 128), lambda l: (l, 0, 0, 0)),
        ],
        out_specs=[
            pl.BlockSpec((1, 2, 2, HEADS, WIN * WIN), lambda l: (l, 0, 0, 0, 0)),
            pl.BlockSpec((1, C, 3 * C), lambda l: (l, 0, 0)),
            pl.BlockSpec((1, C, C), lambda l: (l, 0, 0)),
        ],
        compiler_params=pltpu.CompilerParams(vmem_limit_bytes=VMEM_LIMIT),
    )(tiles, wtiles)


def to_cells(grid):
    return grid.reshape(48, 12, C)


def shards(tokens, cotangent, w_qkv, w_proj, w_in, w_out, earth_bias):
    load, own, send, recv = _matrices()
    loadt, ownt, recvt, sendt = (jnp.asarray(m.T, BF16) for m in (load, own, recv, send))
    load, own, send, recv = (jnp.asarray(m, BF16) for m in (load, own, send, recv))
    params = [w_qkv, w_proj, w_in, w_out.transpose(0, 2, 1)]
    tok, wide = ((TOK, C), BF16), ((TOK, 3 * C), BF16)
    qkvt, mixedt = ((4, 3 * C, WIN), BF16), ((4, C, WIN), BF16)
    prob = ((24, WIN, WIN), BF16)
    spread = [((WIN * 8, 128), F32)] * 2
    back = [tok, tok, ((3 * C, WIN), BF16), tok, ((C, FF), F32), ((WIN * 24, 128), F32), ((WIN * 24, 128), F32)]
    sums = [((256, 16, 128), BF16), ((80, 16, 128), BF16)]

    *state, kept, sent = compute_call(
        forward_kernel,
        [to_cells(tokens), to_cells(cotangent), load, own, send] + [(p, 0) for p in params + [earth_bias]],
        [tok, tok, qkvt, prob, mixedt, tok, ((TOK, FF), BF16), ((2, TOK, C), BF16), ((2, SEND, C), BF16)],
        [wide, tok] + spread + [((768, C), BF16)],
    )
    arrived = exchange(sent, -1, 0)
    kept, sent, tiles1, wtiles1 = compute_call(
        middle_kernel,
        [kept, arrived, recv, ownt, recvt] + [(p, 1) for p in params + [earth_bias]],
        [tok, ((1, SEND, C), BF16)] + sums,
        [tok, wide, qkvt, prob, mixedt, tok] + back + spread,
    )
    arrived = exchange(sent, 1, 1)
    grid, tiles0, wtiles0 = compute_call(
        backward_kernel,
        [kept, arrived, sendt, loadt] + state + [(p, 0) for p in params],
        [((48, 12, C), BF16)] + sums,
        back,
    )
    tiles, wtiles = sum_all(tiles0.reshape(ROWS, 128), tiles1.reshape(ROWS, 128), wtiles0, wtiles1)
    bias_grad, qkv_grad, proj_grad = unpack(tiles, wtiles)
    grid = grid.reshape(4, 12, 12, C)
    return grid, qkv_grad, proj_grad, bias_grad


def solution(mesh):
    return jax.shard_map(
        shards,
        mesh=mesh,
        in_specs=(
            P(None, "lat", "lon", None),
            P(None, "lat", "lon", None),
            P(),
            P(),
            P(),
            P(),
            P(None, None, "lat", None, None),
        ),
        out_specs=(P(None, "lat", "lon", None), P(), P(), P(None, None, "lat", None, None)),
        check_vma=False,
    )
```

time: 199 us -> 206 us (1.035)
  local copies, waits for them, and re-layouts: 16.1 us -> 31.6 us
  Pallas kernels: 181 us -> 172 us
    unnamed x8 -> x67, local copies, waits for them, and re-layouts: 16.1 us -> 31.6 us
    pallas_call x3, Pallas kernels: 74 us -> 68.6 us  [compute_call(): pl.pallas_call(kernel, out_shape=[jax.ShapeDtypeStruct(shape, kind) for s...]
    pallas_call x1, Pallas kernels: 74.3 us -> 71.5 us  [sum_all(): pl.pallas_call(sum_kernel, out_shape=[jax.ShapeDtypeStruct((2, ROWS, 128)...]
where the time goes in v1:
time: 206 us; the launch traced here: 204 us
  Pallas kernels  172 us (83%)
  local copies, waits for them, and re-layouts  31.6 us (15%)
    pallas_call x1, Pallas kernels, sum_all(): pl.pallas_call(sum_kernel, out_shape=[jax.ShapeDtypeStruct((2, ROWS, 128)...  71.5 us
    pallas_call x3, Pallas kernels, compute_call(): pl.pallas_call(kernel, out_shape=[jax.ShapeDtypeStruct(shape, kind) for s...  68.6 us
    unnamed x67, local copies, waits for them, and re-layouts  31.6 us
    pallas_call x2, Pallas kernels, exchange(): pl.pallas_call(functools.partial(exchange_kernel, sign), out_shape=jax.Sh...  28.7 us

profile of v1, /device:TPU:8, one launch (start us, length us, event | category | flops | bytes accessed | tf_op | source)
XLA Modules:
  0.0 204.3 jit_solution(17660521347533993924)
XLA Ops:
  0.6 1.0 copy.19
  1.6 1.0 copy.20
  2.7 0.0 copy-start
  2.7 0.0 copy-start.1
  2.7 0.0 copy-start.2
  2.7 0.0 copy-start.3
  2.7 0.0 copy-start.10
  2.7 0.0 copy-start.13
  2.7 3.5 %copy.21.bias_ref = bf16[2,2,2,6,20736]{4,3,2,1,0:T(8,128)(2,1)} copy(bf16[2,2,2,6,20736]{4,2,3,1,0:T(2,128)(2,1)} %param.21) | data formatting | bytes 3981312 | tf_op args[6]
  6.2 0.0 copy-done
  6.2 0.0 copy-done.1
  6.2 0.0 copy-done.2
  6.2 0.0 copy-done.3
  6.2 0.0 copy-done.10
  6.2 0.0 copy-done.13
  6.2 0.0 copy-start.9
  6.3 20.4 %shard_map.174 = (bf16[576,192]{1,0:T(8,128)(2,1)S(1)}, bf16[576,192]{1,0:T(8,128)(2,1)S(1)}, bf16[4,576,144]{2,1,0:T(8,128)(2,1)}, bf16[24,144,144]{2,1,0:T(8,1...) custom-call(bf16[48,12,192]{2,1,0:T(8,128)(2,1)S(1)} %bitcast.9, ...), custom_call_target="tpu_custom_call" | custom-call | tf_op jit(solution)/shard_map/pallas_call | solution.py:621
  26.7 0.0 copy-start.11
  26.7 0.8 copy-done.11
  27.5 0.0 copy-start.17
  27.5 0.7 copy-done.17
  28.2 0.0 copy-start.19
  28.2 0.7 copy-done.19
  29.0 0.0 copy-start.22
  29.0 0.7 copy-done.22
  29.7 0.0 copy-start.24
  29.7 0.7 copy-done.24
  30.4 0.0 copy-start.26
  30.4 0.7 copy-done.26
  31.1 15.6 %shard_map.175.arrived = bf16[2,384,192]{2,1,0:T(8,128)(2,1)} custom-call(bf16[2,384,192]{2,1,0:T(8,128)(2,1)} %copy-done.19), custom_call_target="tpu_custom_call" | custom-call | tf_op jit(solution)/shard_map/pallas_call | solution.py:286
  46.7 0.0 copy-done.9
  46.7 0.0 copy-start.4
  46.7 1.0 copy-done.4
  47.7 0.0 copy-start.12
  47.7 1.1 copy-done.12
  48.8 0.0 copy-start.14
  48.8 1.0 copy-done.14
  49.8 0.0 copy-start.15
  49.8 1.0 copy-done.15
  50.8 0.0 copy-start.7
  50.8 32.3 %shard_map.176 = (bf16[576,192]{1,0:T(8,128)(2,1)S(1)}, bf16[1,384,192]{2,1,0:T(8,128)(2,1)S(1)}, bf16[256,16,128]{2,1,0:T(8,128)(2,1)}, bf16[80,16,128]{2,1,0:T(8,128)(2,1)S(1)}) custom-call(bf16[2,576,192]{2,1,0:T(8,128)(2,1)S(1)} %copy-done.12, bf16[2,384,192]{2,1,0:T(8,128)(2,1)S(1)} %copy-done.4, bf16[576,384]{1,0:T(8,128)(2,1)S(1)} %copy-done.15, ...), custom_call_target="tpu_custom_call" | custom-call | tf_op jit(solution)/shard_map/pallas_call | solution.py:621
  83.1 0.0 copy-start.20
  83.1 0.7 copy-done.20
  83.9 0.0 copy-start.28
  83.9 0.7 copy-done.28
  84.6 0.7 copy-done.30
  85.3 13.2 %shard_map.177.arrived = bf16[1,384,192]{2,1,0:T(8,128)(2,1)} custom-call(bf16[1,384,192]{2,1,0:T(8,128)(2,1)} %copy-done.30), custom_call_target="tpu_custom_call" | custom-call | tf_op jit(solution)/shard_map/pallas_call | solution.py:286
  98.4 0.0 copy-done.7
  98.4 0.0 copy-start.8
  98.5 0.9 copy-done.8
  99.4 1.0 copy-done.16
  100.4 1.0 copy-done.18
  101.4 1.0 copy-done.23
  102.3 1.0 copy-done.25
  103.3 1.0 copy-done.27
  104.3 1.0 copy-done.29
  105.2 15.9 %shard_map.178 = (bf16[48,12,192]{2,1,0:T(8,128)(2,1)S(1)}, bf16[256,16,128]{2,1,0:T(8,128)(2,1)}, bf16[80,16,128]{2,1,0:T(8,128)(2,1)S(1)}) custom-call(bf16[576,192]{1,0:T(8,128)(2,1)S(1)} %copy-done.29, bf16[1,384,192]{2,1,0:T(8,128)(2,1)S(1)} %copy-done.8, bf16[576,384]{1,0:T(8,128)(2,1)S(1)} %copy-done.16, bf16[768,576]{1,0:T(8,128)(2,1)} %constant.16.clone.loadt_ref, ...), custom_call_target="tpu_custom_call" | custom-call | tf_op jit(solution)/shard_map/pallas_call | solution.py:621
  121.2 0.9 copy.23
  122.1 0.0 copy-done.5
  122.1 0.0 copy-done.21
  122.1 1.2 copy-done.6
  123.3 71.5 %shard_map.179 = (bf16[2,4096,128]{2,1,0:T(8,128)(2,1)S(1)}, bf16[2,80,16,128]{3,2,1,0:T(8,128)(2,1)S(1)}) custom-call(bf16[4096,128]{1,0:T(8,128)(2,1)S(1)} %bitcast.12, bf16[4096,128]{1,0:T(8,128)(2,1)S(1)} %bitcast.11, bf16[80,16,128]{2,1,0:T(8,128)(2,1)S(1)} %get-tuple-element.39.wtiles0, bf16[80,16,128]{2,1,0:T(8,128)(2,1)S(1)} %copy-done.21), custom_call_target="tpu_custom_call" | custom-call | tf_op jit(solution)/shard_map/pallas_call | solution.py:663
  194.8 2.9 %shard_map.180 = (f32[2,2,2,6,20736]{4,3,2,1,0:T(8,128)}, f32[2,192,576]{2,1,0:T(8,128)}, f32[2,192,192]{2,1,0:T(8,128)}) custom-call(bf16[2,4096,128]{2,1,0:T(8,128)(2,1)S(1)} %get-tuple-element.41.tiles_ref, bf16[2,80,16,128]{3,2,1,0:T(8,128)(2,1)S(1)} %get-tuple-element.42.wtiles_ref), custom_call_target="tpu_custom_call" | custom-call | tf_op jit(solution)/shard_map/pallas_call | solution.py:707
  197.8 6.5 %copy.24 = f32[2,2,2,6,20736]{4,2,3,1,0:T(2,128)} copy(f32[2,2,2,6,20736]{4,3,2,1,0:T(8,128)} %get-tuple-element.49) | data formatting | bytes 7962624
  (10 shorter events, 0.0 us)
Async XLA Ops:
  2.7 3.5 %copy-start = (bf16[2,192,768]{2,1,0:T(8,128)(2,1)S(1)}, bf16[2,192,768]{2,1,0:T(8,128)(2,1)}, u32[]{:S(2)}) copy-start(bf16[2,192,768]{2,1,0:T(8,128)(2,1)} %w_in.5) | copy-start | bytes 1769476
  2.7 3.5 %copy-start.1 = (bf16[2,768,192]{1,2,0:T(8,128)(2,1)S(1)}, bf16[2,768,192]{1,2,0:T(8,128)(2,1)}, u32[]{:S(2)}) copy-start(bf16[2,768,192]{1,2,0:T(8,128)(2,1)} %param.20) | copy-start | bytes 1769476
  2.7 3.5 %copy-start.2 = (bf16[2,192,576]{2,1,0:T(8,128)(2,1)S(1)}, bf16[2,192,576]{2,1,0:T(8,128)(2,1)}, u32[]{:S(2)}) copy-start(bf16[2,192,576]{2,1,0:T(8,128)(2,1)} %w_qkv.5) | copy-start | bytes 1327108
  2.7 3.5 %copy-start.3 = (bf16[2,192,192]{2,1,0:T(8,128)(2,1)S(1)}, bf16[2,192,192]{2,1,0:T(8,128)(2,1)}, u32[]{:S(2)}) copy-start(bf16[2,192,192]{2,1,0:T(8,128)(2,1)} %w_proj.5) | copy-start | bytes 442372
  2.7 3.5 %copy-start.10 = (bf16[576,576]{1,0:T(8,128)(2,1)S(1)}, bf16[576,576]{1,0:T(8,128)(2,1)}, u32[]{:S(2)}) copy-start(bf16[576,576]{1,0:T(8,128)(2,1)} %constant.21.clone.own_ref) | copy-start | bytes 1990660
  2.7 3.5 %copy-start.13 = (bf16[384,576]{1,0:T(8,128)(2,1)S(1)}, bf16[384,576]{1,0:T(8,128)(2,1)}, u32[]{:S(2)}) copy-start(bf16[384,576]{1,0:T(8,128)(2,1)} %constant.22.clone.send_ref) | copy-start | bytes 1327108
  6.2 40.5 %copy-start.9 = (bf16[576,576]{1,0:T(8,128)(2,1)S(1)}, bf16[576,576]{1,0:T(8,128)(2,1)}, u32[]{:S(2)}) copy-start(bf16[576,576]{1,0:T(8,128)(2,1)} %constant.17.clone.ownt_ref) | copy-start | bytes 1990660
  26.7 0.8 copy-start.11
  27.5 0.7 copy-start.17
  28.2 0.7 copy-start.19
  29.0 0.7 copy-start.22
  29.7 0.7 copy-start.24
  30.4 0.7 copy-start.26
  46.7 1.0 copy-start.4
  47.7 1.1 copy-start.12
  48.8 1.0 copy-start.14
  49.8 1.0 copy-start.15
  50.8 47.6 %copy-start.7 = (bf16[576,768]{1,0:T(8,128)(2,1)S(1)}, bf16[576,768]{1,0:T(8,128)(2,1)}, u32[]{:S(2)}) copy-start(bf16[576,768]{1,0:T(8,128)(2,1)} %get-tuple-element.35.slope) | copy-start | bytes 2654212
  83.1 0.7 copy-start.20
  83.9 0.7 copy-start.28
  84.6 0.7 copy-start.30
  98.4 0.9 copy-start.8
  99.4 1.0 copy-start.16
  100.4 1.0 copy-start.18
  101.4 1.0 copy-start.23
  102.3 1.0 copy-start.25
  103.3 1.0 copy-start.27
  104.3 1.0 copy-start.29
  105.2 16.9 %copy-start.5 = (bf16[256,16,128]{2,1,0:T(8,128)(2,1)S(1)}, bf16[256,16,128]{2,1,0:T(8,128)(2,1)}, u32[]{:S(2)}) copy-start(bf16[256,16,128]{2,1,0:T(8,128)(2,1)} %get-tuple-element.38) | copy-start | bytes 3145732
  105.2 16.9 %copy-start.21 = (bf16[80,16,128]{2,1,0:T(8,128)(2,1)S(1)}, bf16[80,16,128]{2,1,0:T(8,128)(2,1)}, u32[]{:S(2)}) copy-start(bf16[80,16,128]{2,1,0:T(8,128)(2,1)} %copy-done.20) | copy-start | bytes 983044
  122.1 1.2 copy-start.6

commit v2 on v1

--- a/solution.py
+++ b/solution.py
@@ -20,7 +20,7 @@
 SCALE = HD ** (-0.5)
 MESH = pl.DeviceIdType.MESH
 E0, S0, D0, SEND = 0, 224, 304, 384
-VMEM_LIMIT = 48 * 1024 * 1024
+VMEM_LIMIT = 56 * 1024 * 1024
 ZS = 8
 PAIRS = 12
 FLAT = 3888
@@ -33,7 +33,7 @@
 
 
 def _matrices():
-    load = np.zeros((TOK, 768), np.float32)
+    load = np.zeros((TOK, TOK), np.float32)
     own = np.zeros((TOK, TOK), np.float32)
     send = np.zeros((SEND, TOK), np.float32)
     recv = np.zeros((TOK, SEND), np.float32)
@@ -41,7 +41,7 @@
         for row in range(12):
             for col in range(12):
                 here = _plain_index(level, row, col)
-                load[here, (level * 12 + row) * 16 + col] = 1
+                load[here, (row * 12 + col) * 4 + level] = 1
                 target_row, target_col = row - 3, col - 6
                 target = _plain_index((level - 1) % 4, target_row % 12, target_col % 12)
                 if target_row >= 0 and target_col >= 0:
@@ -504,10 +504,15 @@
         next(stream, None)
 
 
-def drain(*streams):
-    live = list(streams)
-    while live:
-        live = [stream for stream in live if next(stream, live) is not live]
+def drain(fast, slow, rounds):
+    step = 0
+    while fast:
+        fast = [stream for stream in fast if next(stream, 1) is None]
+        if step in rounds:
+            advance(*slow)
+        step += 1
+    while slow:
+        slow = [stream for stream in slow if next(stream, 1) is None]
 
 
 def attention_block(x, source, qkv, qkvt, prob, mixedt, mixed, w_qkv, w_proj, w_in, biases, masked):
@@ -528,22 +533,15 @@
     return middle, pre, phi, phi + pre * density(pre)
 
 
-def load_grid(grid_ref, pad, matrix):
-    for i in range(48):
-        pad[16 * i : 16 * i + 12, :] = grid_ref[i]
-    return nn(matrix, pad[...])
-
-
 def forward_kernel(
     tok_ref, cot_ref, load_ref, own_ref, send_ref, w_qkv, w_proj, w_in, w_outt, bias_ref,
     x_out, source, qkvt, prob, mixedt, mid_out, slope_out, kept, sent,
-    qkv, mixed, main, rest, pad,
+    qkv, mixed, main, rest,
 ):
-    pad[...] = jnp.zeros_like(pad)
-    cot = load_grid(cot_ref, pad, load_ref[...]).astype(BF16)
+    cot = nn(load_ref[...], cot_ref[...].reshape(TOK, C)).astype(BF16)
     sent[1] = nn(send_ref[...], cot).astype(BF16)
     kept[1] = nn(own_ref[...], cot).astype(BF16)
-    x0 = load_grid(tok_ref, pad, load_ref[...])
+    x0 = nn(load_ref[...], tok_ref[...].reshape(TOK, C))
     x_out[...] = x0.astype(BF16)
     middle, pre, phi, slope = attention_block(
         x0, source, qkv, qkvt, prob, mixedt, mixed, w_qkv, w_proj, w_in, (bias_ref, main, rest), False
@@ -602,9 +600,7 @@
 
     lax.fori_loop(0, 4, back, 0)
     result = (mgrad[...].astype(F32) + norm_back(x_ref[...].astype(F32), sgrad[...].astype(F32))).astype(BF16)
-    placed = nn(loadt_ref[...], result).astype(BF16)
-    for i in range(48):
-        grid_out[i] = placed[16 * i : 16 * i + 12, :]
+    grid_out[...] = nn(loadt_ref[...], result).astype(BF16).reshape(144, 4, C)
     pack_bias(main24, rest24, tiles)
     pack_weights(wgrad, wtiles)
 
@@ -651,7 +647,7 @@
                 wdone.at[layer], w_sems.at[layer], 8 * layer,
             )
         )
-    drain(*streams)
+    drain(streams[::2], streams[1::2], (0, 2, 5, 7))
 
 
 def sum_all(tiles0, tiles1, wtiles0, wtiles1):
@@ -726,7 +722,7 @@
 
 
 def to_cells(grid):
-    return grid.reshape(48, 12, C)
+    return grid.transpose(1, 2, 0, 3).reshape(144, 4, C)
 
 
 def shards(tokens, cotangent, w_qkv, w_proj, w_in, w_out, earth_bias):
@@ -745,7 +741,7 @@
         forward_kernel,
         [to_cells(tokens), to_cells(cotangent), load, own, send] + [(p, 0) for p in params + [earth_bias]],
         [tok, tok, qkvt, prob, mixedt, tok, ((TOK, FF), BF16), ((2, TOK, C), BF16), ((2, SEND, C), BF16)],
-        [wide, tok] + spread + [((768, C), BF16)],
+        [wide, tok] + spread,
     )
     arrived = exchange(sent, -1, 0)
     kept, sent, tiles1, wtiles1 = compute_call(
@@ -758,12 +754,12 @@
     grid, tiles0, wtiles0 = compute_call(
         backward_kernel,
         [kept, arrived, sendt, loadt] + state + [(p, 0) for p in params],
-        [((48, 12, C), BF16)] + sums,
+        [((144, 4, C), BF16)] + sums,
         back,
     )
     tiles, wtiles = sum_all(tiles0.reshape(ROWS, 128), tiles1.reshape(ROWS, 128), wtiles0, wtiles1)
     bias_grad, qkv_grad, proj_grad = unpack(tiles, wtiles)
-    grid = grid.reshape(4, 12, 12, C)
+    grid = grid.reshape(12, 12, 4, C).transpose(2, 0, 1, 3)
     return grid, qkv_grad, proj_grad, bias_grad
 
 

time: 206 us -> 186 us (0.903)
  local copies, waits for them, and re-layouts: 31.6 us -> 9.81 us
  Pallas kernels: 172 us -> 175 us
    unnamed x67 -> x2, local copies, waits for them, and re-layouts: 31.6 us -> 9.81 us
    pallas_call x3, Pallas kernels: 68.6 us -> 72.4 us  [compute_call(): pl.pallas_call(kernel, out_shape=[jax.ShapeDtypeStruct(shape, kind) for s...]
where the time goes in v2:
time: 186 us; the launch traced here: 185 us
  Pallas kernels  175 us (94%)
  local copies, waits for them, and re-layouts  9.81 us (5%)
    pallas_call x3, Pallas kernels, compute_call(): pl.pallas_call(kernel, out_shape=[jax.ShapeDtypeStruct(shape, kind) for s...  72.4 us
    pallas_call x1, Pallas kernels, sum_all(): pl.pallas_call(sum_kernel, out_shape=[jax.ShapeDtypeStruct((2, ROWS, 128)...  69.5 us
    pallas_call x2, Pallas kernels, exchange(): pl.pallas_call(functools.partial(exchange_kernel, sign), out_shape=jax.Sh...  28.8 us
    unnamed x2, local copies, waits for them, and re-layouts  9.81 us
    pallas_call x1, Pallas kernels, unpack(): pl.pallas_call(unpack_kernel, grid=(2,), out_shape=[jax.ShapeDtypeStruct(...  4.18 us

profile of v2, /device:TPU:8, one launch (start us, length us, event | category | flops | bytes accessed | tf_op | source)
XLA Modules:
  0.0 185.2 jit_solution(14400048191048030117)
XLA Ops:
  0.6 3.3 %copy.19.bias_ref = bf16[2,2,2,6,20736]{4,3,2,1,0:T(8,128)(2,1)} copy(bf16[2,2,2,6,20736]{4,2,3,1,0:T(2,128)(2,1)} %param.21) | data formatting | bytes 3981312 | tf_op args[6]
  3.9 22.0 %shard_map.174 = (bf16[576,192]{1,0:T(8,128)(2,1)}, bf16[576,192]{1,0:T(8,128)(2,1)}, bf16[4,576,144]{2,1,0:T(8,128)(2,1)}, bf16[24,144,144]{2,1,0:T(8,128)(2,1)...) custom-call(bf16[144,4,192]{2,1,0:T(4,128)(2,1)} %bitcast.17, ...), custom_call_target="tpu_custom_call" | custom-call | tf_op jit(solution)/shard_map/pallas_call | solution.py:617
  26.0 15.6 %shard_map.175.arrived = bf16[2,384,192]{2,1,0:T(8,128)(2,1)} custom-call(bf16[2,384,192]{2,1,0:T(8,128)(2,1)} %get-tuple-element.26.send_ref), custom_call_target="tpu_custom_call" | custom-call | tf_op jit(solution)/shard_map/pallas_call | solution.py:286
  41.6 33.5 %shard_map.176 = (bf16[576,192]{1,0:T(8,128)(2,1)}, bf16[1,384,192]{2,1,0:T(8,128)(2,1)}, bf16[256,16,128]{2,1,0:T(8,128)(2,1)}, bf16[80,16,128]{2,1,0:T(8,128)(2,1)}) custom-call(bf16[2,576,192]{2,1,0:T(8,128)(2,1)} %get-tuple-element.25.kept, bf16[2,384,192]{2,1,0:T(8,128)(2,1)} %shard_map.175.arrived, bf16[576,384]{1,0:T(8,128)(2,1)} %constant.23.clone.recv_ref, ...), custom_call_target="tpu_custom_call" | custom-call | tf_op jit(solution)/shard_map/pallas_call | solution.py:617
  75.1 13.2 %shard_map.177.arrived = bf16[1,384,192]{2,1,0:T(8,128)(2,1)} custom-call(bf16[1,384,192]{2,1,0:T(8,128)(2,1)} %get-tuple-element.28.send_ref), custom_call_target="tpu_custom_call" | custom-call | tf_op jit(solution)/shard_map/pallas_call | solution.py:286
  88.3 16.8 %shard_map.178 = (bf16[144,4,192]{2,1,0:T(4,128)(2,1)}, bf16[256,16,128]{2,1,0:T(8,128)(2,1)}, bf16[80,16,128]{2,1,0:T(8,128)(2,1)}) custom-call(bf16[576,192]{1,0:T(8,128)(2,1)} %get-tuple-element.27.kept, bf16[1,384,192]{2,1,0:T(8,128)(2,1)} %shard_map.177.arrived, bf16[576,384]{1,0:T(8,128)(2,1)} %constant.19.clone.sendt_ref, ...), custom_call_target="tpu_custom_call" | custom-call | tf_op jit(solution)/shard_map/pallas_call | solution.py:617
  105.1 69.5 %shard_map.179 = (bf16[2,4096,128]{2,1,0:T(8,128)(2,1)}, bf16[2,80,16,128]{3,2,1,0:T(8,128)(2,1)}) custom-call(bf16[4096,128]{1,0:T(8,128)(2,1)} %bitcast.16, bf16[4096,128]{1,0:T(8,128)(2,1)} %bitcast.15, bf16[80,16,128]{2,1,0:T(8,128)(2,1)} %get-tuple-element.39.wtiles0, bf16[80,16,128]{2,1,0:T(8,128)(2,1)} %get-tuple-element.40.wtiles1), custom_call_target="tpu_custom_call" | custom-call | tf_op jit(solution)/shard_map/pallas_call | solution.py:659
  174.6 4.2 %shard_map.180 = (f32[2,2,2,6,20736]{4,3,2,1,0:T(8,128)}, f32[2,192,576]{2,1,0:T(8,128)}, f32[2,192,192]{2,1,0:T(8,128)}) custom-call(bf16[2,4096,128]{2,1,0:T(8,128)(2,1)} %get-tuple-element.41.tiles_ref, bf16[2,80,16,128]{3,2,1,0:T(8,128)(2,1)} %get-tuple-element.42.wtiles_ref), custom_call_target="tpu_custom_call" | custom-call | tf_op jit(solution)/shard_map/pallas_call | solution.py:703
  178.7 6.5 %copy.21 = f32[2,2,2,6,20736]{4,2,3,1,0:T(2,128)} copy(f32[2,2,2,6,20736]{4,3,2,1,0:T(8,128)} %get-tuple-element.49) | data formatting | bytes 7962624

commit v3 on v2

--- a/solution.py
+++ b/solution.py
@@ -103,24 +103,27 @@
     return pl.ds(pl.multiple_of(window * WIN, WIN), WIN)
 
 
-def spread_bias(bias_ref, window, main, rest):
-    def step(group, carry):
-        block = bias_ref[
-            0, window // 2, window % 2, :, pl.ds(pl.multiple_of(group * 1152, 128), 1152)
-        ].astype(F32)
-        for r in range(8):
-            at = pl.ds(pl.multiple_of(group * 64, 64) + 8 * r, 6)
-            main[at, :] = block[:, WIN * r : WIN * r + 128]
-            rest[at, 0:16] = block[:, WIN * r + 128 : WIN * r + WIN]
-        return carry
-
-    lax.fori_loop(0, 18, step, 0)
-
-
-def head_bias(main, rest, head):
-    left = main[pl.ds(head, WIN, stride=8), :]
-    right = rest[pl.ds(head, WIN, stride=8), :]
-    return jnp.concatenate([left, right[:, :16]], axis=1)
+def spread_bias(bias_ref, layer, lined, table):
+    for window in range(4):
+        for j in range(162):
+            row = window * 18 + j // 9
+            value = bias_ref[layer, window // 2, window % 2, :, 128 * j : 128 * j + 128]
+            lined[row, j % 9 * 8 : j % 9 * 8 + HEADS, :] = value.astype(F32)
+    rows = lax.broadcasted_iota(jnp.int32, (256, 256), 0)
+    cols = lax.broadcasted_iota(jnp.int32, (256, 256), 1)
+    for r in range(8):
+        pick = jnp.where(jnp.logical_and(rows - cols == 16 * r, cols < WIN), 1.0, 0.0).astype(BF16)
+        pair = [lined[:, 8 * (r + i) : 8 * (r + i) + 8, :].reshape(576, 128) for i in range(2)]
+        placed = nn(jnp.concatenate(pair, axis=1).astype(BF16), pick)
+        for part in range(2):
+            half = placed[:, 128 * part : 128 * part + 128]
+            for row in range(72):
+                table[part][64 * row + 8 * r : 64 * row + 8 * r + 8, :] = half[8 * row : 8 * row + 8]
+
+
+def head_bias(table, window, head):
+    at = pl.ds(pl.multiple_of(window * WIN * 8, 8) + head, WIN, stride=8)
+    return jnp.concatenate([table[0][at, :], table[1][at, :][:, 0:16]], axis=1)
 
 
 def pack_bias(main, rest, out_ref):
@@ -155,15 +158,14 @@
 
 
 def attention_forward(window, qkv_ref, qkvt_ref, prob_ref, mixedt_ref, mixed_ref, biases, mask):
-    bias_ref, main, rest = biases
-    spread_bias(bias_ref, window, main, rest)
+
     qkv = qkv_ref[rows_of(window), :]
     qkvt_ref[window] = flip(qkv, 3 * C)
     for head in range(HEADS):
         lo = head * HD
         keys = qkvt_ref[window, C + lo : C + lo + HD, :]
         values = qkvt_ref[window, 2 * C + lo : 2 * C + lo + HD, :]
-        scores = nn(qkv[:, lo : lo + HD], keys) * SCALE + head_bias(main, rest, head)
+        scores = nn(qkv[:, lo : lo + HD], keys) * SCALE + head_bias(biases, window, head)
         weights = jnp.exp(scores)
         if mask is not None:
             weights = weights * mask
@@ -536,15 +538,17 @@
 def forward_kernel(
     tok_ref, cot_ref, load_ref, own_ref, send_ref, w_qkv, w_proj, w_in, w_outt, bias_ref,
     x_out, source, qkvt, prob, mixedt, mid_out, slope_out, kept, sent,
-    qkv, mixed, main, rest,
+    qkv, mixed, main, rest, lined,
 ):
     cot = nn(load_ref[...], cot_ref[...].reshape(TOK, C)).astype(BF16)
     sent[1] = nn(send_ref[...], cot).astype(BF16)
     kept[1] = nn(own_ref[...], cot).astype(BF16)
     x0 = nn(load_ref[...], tok_ref[...].reshape(TOK, C))
     x_out[...] = x0.astype(BF16)
+    lined[...] = jnp.zeros_like(lined)
+    spread_bias(bias_ref, 0, lined, (main, rest))
     middle, pre, phi, slope = attention_block(
-        x0, source, qkv, qkvt, prob, mixedt, mixed, w_qkv, w_proj, w_in, (bias_ref, main, rest), False
+        x0, source, qkv, qkvt, prob, mixedt, mixed, w_qkv, w_proj, w_in, (main, rest), False
     )
     mid_out[...] = middle
     slope_out[...] = slope.astype(BF16)
@@ -556,11 +560,13 @@
 def middle_kernel(
     kept, arrived, recv_ref, ownt_ref, recvt_ref, w_qkv, w_proj, w_in, w_outt, bias_ref,
     kept_out, sent, tiles, wtiles,
-    source, qkv, qkvt, prob, mixedt, mixed, mgrad, grad, gradt, sgrad, wgrad, main24, rest24, main, rest,
+    source, qkv, qkvt, prob, mixedt, mixed, mgrad, grad, gradt, sgrad, wgrad, main24, rest24, main, rest, lined,
 ):
     x1 = kept[0].astype(F32) + nn(recv_ref[...], arrived[0])
+    lined[...] = jnp.zeros_like(lined)
+    spread_bias(bias_ref, 0, lined, (main, rest))
     middle, _, _, slope = attention_block(
-        x1, source, qkv, qkvt, prob, mixedt, mixed, w_qkv, w_proj, w_in, (bias_ref, main, rest), True
+        x1, source, qkv, qkvt, prob, mixedt, mixed, w_qkv, w_proj, w_in, (main, rest), True
     )
     cot = (kept[1].astype(F32) + nn(recv_ref[...], arrived[1])).astype(BF16)
     mgrad[...] = mlp_back(middle, cot, slope, w_in[0], w_outt[0])
@@ -733,7 +739,7 @@
     tok, wide = ((TOK, C), BF16), ((TOK, 3 * C), BF16)
     qkvt, mixedt = ((4, 3 * C, WIN), BF16), ((4, C, WIN), BF16)
     prob = ((24, WIN, WIN), BF16)
-    spread = [((WIN * 8, 128), F32)] * 2
+    spread = [((4 * WIN * 8 + 8, 128), F32)] * 2 + [((72, 72, 128), F32)]
     back = [tok, tok, ((3 * C, WIN), BF16), tok, ((C, FF), F32), ((WIN * 24, 128), F32), ((WIN * 24, 128), F32)]
     sums = [((256, 16, 128), BF16), ((80, 16, 128), BF16)]
 

time: 186 us -> 175 us (0.941)
  Pallas kernels: 175 us -> 165 us
    pallas_call x3, Pallas kernels: 72.4 us -> 62 us  [compute_call(): pl.pallas_call(kernel, out_shape=[jax.ShapeDtypeStruct(shape, kind) for s...]
where the time goes in v3:
time: 175 us
  Pallas kernels  165 us (94%)
  local copies, waits for them, and re-layouts  9.81 us (6%)
    pallas_call x1, Pallas kernels, sum_all(): pl.pallas_call(sum_kernel, out_shape=[jax.ShapeDtypeStruct((2, ROWS, 128)...  69.7 us
    pallas_call x3, Pallas kernels, compute_call(): pl.pallas_call(kernel, out_shape=[jax.ShapeDtypeStruct(shape, kind) for s...  62 us
    pallas_call x2, Pallas kernels, exchange(): pl.pallas_call(functools.partial(exchange_kernel, sign), out_shape=jax.Sh...  28.8 us
    unnamed x2, local copies, waits for them, and re-layouts  9.81 us
    pallas_call x1, Pallas kernels, unpack(): pl.pallas_call(unpack_kernel, grid=(2,), out_shape=[jax.ShapeDtypeStruct(...  4.18 us

profile of v3, /device:TPU:8, one launch (start us, length us, event | category | flops | bytes accessed | tf_op | source)
XLA Modules:
  0.0 175.0 jit_solution(13640696859249705245)
XLA Ops:
  0.6 3.3 %copy.19.bias_ref = bf16[2,2,2,6,20736]{4,3,2,1,0:T(8,128)(2,1)} copy(bf16[2,2,2,6,20736]{4,2,3,1,0:T(2,128)(2,1)} %param.21) | data formatting | bytes 3981312 | tf_op args[6]
  3.9 17.5 %shard_map.174 = (bf16[576,192]{1,0:T(8,128)(2,1)}, bf16[576,192]{1,0:T(8,128)(2,1)}, bf16[4,576,144]{2,1,0:T(8,128)(2,1)}, bf16[24,144,144]{2,1,0:T(8,128)(2,1)...) custom-call(bf16[144,4,192]{2,1,0:T(4,128)(2,1)} %bitcast.17, ...), custom_call_target="tpu_custom_call" | custom-call | tf_op jit(solution)/shard_map/pallas_call | solution.py:623
  21.4 15.6 %shard_map.175.arrived = bf16[2,384,192]{2,1,0:T(8,128)(2,1)} custom-call(bf16[2,384,192]{2,1,0:T(8,128)(2,1)} %get-tuple-element.26.send_ref), custom_call_target="tpu_custom_call" | custom-call | tf_op jit(solution)/shard_map/pallas_call | solution.py:288
  37.0 27.6 %shard_map.176 = (bf16[576,192]{1,0:T(8,128)(2,1)}, bf16[1,384,192]{2,1,0:T(8,128)(2,1)}, bf16[256,16,128]{2,1,0:T(8,128)(2,1)}, bf16[80,16,128]{2,1,0:T(8,128)(2,1)}) custom-call(bf16[2,576,192]{2,1,0:T(8,128)(2,1)} %get-tuple-element.25.kept, bf16[2,384,192]{2,1,0:T(8,128)(2,1)} %shard_map.175.arrived, bf16[576,384]{1,0:T(8,128)(2,1)} %constant.23.clone.recv_ref, ...), custom_call_target="tpu_custom_call" | custom-call | tf_op jit(solution)/shard_map/pallas_call | solution.py:623
  64.6 13.2 %shard_map.177.arrived = bf16[1,384,192]{2,1,0:T(8,128)(2,1)} custom-call(bf16[1,384,192]{2,1,0:T(8,128)(2,1)} %get-tuple-element.28.send_ref), custom_call_target="tpu_custom_call" | custom-call | tf_op jit(solution)/shard_map/pallas_call | solution.py:288
  77.8 16.9 %shard_map.178 = (bf16[144,4,192]{2,1,0:T(4,128)(2,1)}, bf16[256,16,128]{2,1,0:T(8,128)(2,1)}, bf16[80,16,128]{2,1,0:T(8,128)(2,1)}) custom-call(bf16[576,192]{1,0:T(8,128)(2,1)} %get-tuple-element.27.kept, bf16[1,384,192]{2,1,0:T(8,128)(2,1)} %shard_map.177.arrived, bf16[576,384]{1,0:T(8,128)(2,1)} %constant.19.clone.sendt_ref, ...), custom_call_target="tpu_custom_call" | custom-call | tf_op jit(solution)/shard_map/pallas_call | solution.py:623
  94.7 69.7 %shard_map.179 = (bf16[2,4096,128]{2,1,0:T(8,128)(2,1)}, bf16[2,80,16,128]{3,2,1,0:T(8,128)(2,1)}) custom-call(bf16[4096,128]{1,0:T(8,128)(2,1)} %bitcast.16, bf16[4096,128]{1,0:T(8,128)(2,1)} %bitcast.15, bf16[80,16,128]{2,1,0:T(8,128)(2,1)} %get-tuple-element.39.wtiles0, bf16[80,16,128]{2,1,0:T(8,128)(2,1)} %get-tuple-element.40.wtiles1), custom_call_target="tpu_custom_call" | custom-call | tf_op jit(solution)/shard_map/pallas_call | solution.py:665
  164.4 4.2 %shard_map.180 = (f32[2,2,2,6,20736]{4,3,2,1,0:T(8,128)}, f32[2,192,576]{2,1,0:T(8,128)}, f32[2,192,192]{2,1,0:T(8,128)}) custom-call(bf16[2,4096,128]{2,1,0:T(8,128)(2,1)} %get-tuple-element.41.tiles_ref, bf16[2,80,16,128]{3,2,1,0:T(8,128)(2,1)} %get-tuple-element.42.wtiles_ref), custom_call_target="tpu_custom_call" | custom-call | tf_op jit(solution)/shard_map/pallas_call | solution.py:709
  168.6 6.5 %copy.21 = f32[2,2,2,6,20736]{4,2,3,1,0:T(2,128)} copy(f32[2,2,2,6,20736]{4,3,2,1,0:T(8,128)} %get-tuple-element.49) | data formatting | bytes 7962624

commit v4 on v3

--- a/solution.py
+++ b/solution.py
@@ -142,11 +142,12 @@
                 [top[8 * third : 8 * third + 8], bottom[8 * third : 8 * third + 8]], axis=0
             ).astype(BF16)
             for j in range(9):
-                out_ref[third * 81 + group * 9 + j] = both[:, 128 * j : 128 * j + 128]
+                at = pl.multiple_of((third * 81 + group * 9 + j) * 16, 16)
+                out_ref[pl.ds(at, 16), :] = both[:, 128 * j : 128 * j + 128]
         return carry
 
     lax.fori_loop(0, 9, step, 0)
-    out_ref[243:256] = jnp.zeros((13, 16, 128), BF16)
+    out_ref[FLAT:ROWS, :] = jnp.zeros((ROWS - FLAT, 128), BF16)
 
 
 def pack_weights(wgrad, out_ref):
@@ -248,51 +249,30 @@
     )
 
 
-def wait_all(copies):
-    for copy in copies:
-        copy.wait()
-
-
 def greet():
     barrier = pltpu.get_barrier_semaphore()
     for k in range(1, 16):
         for device in (neighbour(k, 0), neighbour(0, k)):
             pl.semaphore_signal(barrier, inc=1, device_id=device, device_id_type=MESH)
-    pl.semaphore_wait(barrier, 30)
-
-
-def exchange_kernel(sign, send_ref, out_ref, send_sems, recv_sems):
-    barrier = pltpu.get_barrier_semaphore()
+    for k in (-1, 1):
+        pl.semaphore_signal(barrier, inc=1, device_id=neighbour(k, k), device_id_type=MESH)
+    return barrier
+
+
+def halo(src, dst, sign, send, recv):
     steps = [(0, sign, E0, S0), (sign, 0, S0, D0), (sign, sign, D0, SEND)]
-    for lat, lon, _, _ in steps:
-        pl.semaphore_signal(barrier, inc=1, device_id=neighbour(-lat, -lon), device_id_type=MESH)
-    pl.semaphore_wait(barrier, 3)
     copies = []
     for i, (lat, lon, start, stop) in enumerate(steps):
         piece = pl.ds(start, stop - start)
-        copy = pltpu.make_async_remote_copy(
-            src_ref=send_ref.at[:, piece],
-            dst_ref=out_ref.at[:, piece],
-            send_sem=send_sems.at[i],
-            recv_sem=recv_sems.at[i],
-            device_id=neighbour(lat, lon),
-            device_id_type=MESH,
-        )
+        copy = remote(src.at[piece], dst.at[piece], send.at[i], recv.at[i], neighbour(lat, lon))
         copy.start()
         copies.append(copy)
+    return copies
+
+
+def wait_all(copies):
     for copy in copies:
         copy.wait()
-
-
-def exchange(sent, sign, collective_id):
-    return pl.pallas_call(
-        functools.partial(exchange_kernel, sign),
-        out_shape=jax.ShapeDtypeStruct(sent.shape, BF16),
-        in_specs=[pl.BlockSpec(memory_space=pltpu.VMEM)],
-        out_specs=pl.BlockSpec(memory_space=pltpu.VMEM),
-        scratch_shapes=[pltpu.SemaphoreType.DMA((3,)), pltpu.SemaphoreType.DMA((3,))],
-        compiler_params=pltpu.CompilerParams(collective_id=collective_id, has_side_effects=True),
-    )(sent)
 
 
 class Ring:
@@ -517,178 +497,173 @@
         slow = [stream for stream in slow if next(stream, 1) is None]
 
 
-def attention_block(x, source, qkv, qkvt, prob, mixedt, mixed, w_qkv, w_proj, w_in, biases, masked):
-    source[...] = normalize(x)[0].astype(BF16)
-    qkv[...] = nn(source[...], w_qkv[0]).astype(BF16)
-
-    def step(window, carry):
-        attention_forward(
-            window, qkv, qkvt, prob, mixedt, mixed, biases, region_mask(window) if masked else None
-        )
-        return carry
-
-    lax.fori_loop(0, 4, step, 0)
-    attended = nn(mixed[...], w_proj[0]).astype(BF16)
-    middle = (x + attended.astype(F32)).astype(BF16)
-    pre = nn(normalize(middle.astype(F32))[0].astype(BF16), w_in[0])
-    phi = cumulative(pre)
-    return middle, pre, phi, phi + pre * density(pre)
-
-
-def forward_kernel(
-    tok_ref, cot_ref, load_ref, own_ref, send_ref, w_qkv, w_proj, w_in, w_outt, bias_ref,
-    x_out, source, qkvt, prob, mixedt, mid_out, slope_out, kept, sent,
-    qkv, mixed, main, rest, lined,
-):
-    cot = nn(load_ref[...], cot_ref[...].reshape(TOK, C)).astype(BF16)
-    sent[1] = nn(send_ref[...], cot).astype(BF16)
-    kept[1] = nn(own_ref[...], cot).astype(BF16)
-    x0 = nn(load_ref[...], tok_ref[...].reshape(TOK, C))
-    x_out[...] = x0.astype(BF16)
-    lined[...] = jnp.zeros_like(lined)
-    spread_bias(bias_ref, 0, lined, (main, rest))
-    middle, pre, phi, slope = attention_block(
-        x0, source, qkv, qkvt, prob, mixedt, mixed, w_qkv, w_proj, w_in, (main, rest), False
-    )
-    mid_out[...] = middle
-    slope_out[...] = slope.astype(BF16)
-    x1 = (middle.astype(F32) + nt((pre * phi).astype(BF16), w_outt[0])).astype(BF16)
-    sent[0] = nn(send_ref[...], x1).astype(BF16)
-    kept[0] = nn(own_ref[...], x1).astype(BF16)
-
-
-def middle_kernel(
-    kept, arrived, recv_ref, ownt_ref, recvt_ref, w_qkv, w_proj, w_in, w_outt, bias_ref,
-    kept_out, sent, tiles, wtiles,
-    source, qkv, qkvt, prob, mixedt, mixed, mgrad, grad, gradt, sgrad, wgrad, main24, rest24, main, rest, lined,
-):
-    x1 = kept[0].astype(F32) + nn(recv_ref[...], arrived[0])
-    lined[...] = jnp.zeros_like(lined)
-    spread_bias(bias_ref, 0, lined, (main, rest))
-    middle, _, _, slope = attention_block(
-        x1, source, qkv, qkvt, prob, mixedt, mixed, w_qkv, w_proj, w_in, (main, rest), True
-    )
-    cot = (kept[1].astype(F32) + nn(recv_ref[...], arrived[1])).astype(BF16)
-    mgrad[...] = mlp_back(middle, cot, slope, w_in[0], w_outt[0])
-    grad[...] = nt(mgrad[...], w_proj[0]).astype(BF16)
-    wgrad[...] = jnp.zeros_like(wgrad)
-
-    def back(window, carry):
-        attention_backward(
-            window, source, qkvt, prob, mixedt, mgrad, grad, w_qkv[0], w_proj[0], gradt, sgrad, wgrad, (main24, rest24)
-        )
-        return carry
-
-    lax.fori_loop(0, 4, back, 0)
-    result = (mgrad[...].astype(F32) + norm_back(x1, sgrad[...].astype(F32))).astype(BF16)
-    sent[0] = nn(recvt_ref[...], result).astype(BF16)
-    kept_out[...] = nn(ownt_ref[...], result).astype(BF16)
-    pack_bias(main24, rest24, tiles)
-    pack_weights(wgrad, wtiles)
-
-
-def backward_kernel(
-    kept, arrived, sendt_ref, loadt_ref, x_ref, source, qkvt, prob, mixedt, mid, slope,
-    w_qkv, w_proj, w_in, w_outt,
-    grid_out, tiles, wtiles,
-    mgrad, grad, gradt, sgrad, wgrad, main24, rest24,
-):
-    upstream = (kept[...].astype(F32) + nn(sendt_ref[...], arrived[0])).astype(BF16)
-    mgrad[...] = mlp_back(mid[...], upstream, slope[...].astype(F32), w_in[0], w_outt[0])
-    grad[...] = nt(mgrad[...], w_proj[0]).astype(BF16)
-    wgrad[...] = jnp.zeros_like(wgrad)
-
-    def back(window, carry):
-        attention_backward(
-            window, source, qkvt, prob, mixedt, mgrad, grad, w_qkv[0], w_proj[0], gradt, sgrad, wgrad, (main24, rest24)
-        )
-        return carry
-
-    lax.fori_loop(0, 4, back, 0)
-    result = (mgrad[...].astype(F32) + norm_back(x_ref[...].astype(F32), sgrad[...].astype(F32))).astype(BF16)
-    grid_out[...] = nn(loadt_ref[...], result).astype(BF16).reshape(144, 4, C)
-    pack_bias(main24, rest24, tiles)
-    pack_weights(wgrad, wtiles)
-
-
-def compute_call(kernel, operands, outs, scratch):
-    specs, arrays = [], []
-    once = pl.Buffered(1)
-    for operand in operands:
-        array, layer = operand if isinstance(operand, tuple) else (operand, None)
-        arrays.append(array)
-        shape = array.shape if layer is None else (1,) + array.shape[1:]
-        index = (0 if layer is None else layer,) + (0,) * (array.ndim - 1)
-        specs.append(pl.BlockSpec(shape, functools.partial(lambda at, _: at, index), pipeline_mode=once))
-    return pl.pallas_call(
-        kernel,
-        out_shape=[jax.ShapeDtypeStruct(shape, kind) for shape, kind in outs],
-        grid=(1,),
-        in_specs=specs,
-        out_specs=[
-            pl.BlockSpec(shape, functools.partial(lambda at, _: at, (0,) * len(shape)), pipeline_mode=once)
-            for shape, kind in outs
-        ],
-        scratch_shapes=[pltpu.VMEM(shape, kind) for shape, kind in scratch],
-        compiler_params=pltpu.CompilerParams(vmem_limit_bytes=VMEM_LIMIT),
-    )(*arrays)
-
-
-def sum_kernel(
-    tiles0, tiles1, wtiles0, wtiles1, bias_out, w_out,
-    a_right_in, a_left_in, a_right_sum, a_left_sum, mine, other,
+def kernel(
+    tok_ref, cot_ref, load_ref, own_ref, send_ref, recv_ref, loadt_ref, ownt_ref, recvt_ref, sendt_ref,
+    w_qkv, w_proj, w_in, w_outt, bias_ref,
+    grid_out, bias_out, w_out,
+    x0_s, source, qkv, qkvt, prob, mixedt, mixed, mid_s, slope_s, mgrad, grad, gradt, sgrad, wgrad,
+    main24, rest24, lined, main, rest, tiles, wtiles, sent, arrived,
+    halo_sems, a_right_in, a_left_in, a_right_sum, a_left_sum, mine, other,
     b_right_in, b_left_in, b_right_sum, b_left_sum, half, half_in, ring_sems, y_sems,
     wpart, wmid, wowned, wdone, w_sems,
 ):
-    greet()
-    streams = []
-    for layer, (tiles, wtiles) in enumerate(((tiles0, wtiles0), (tiles1, wtiles1))):
+    barrier = greet()
+    lined[...] = jnp.zeros_like(lined)
+
+    def forward(x, layer, masked):
+        source[layer] = normalize(x)[0].astype(BF16)
+        qkv[...] = nn(source[layer], w_qkv[layer]).astype(BF16)
+        spread_bias(bias_ref, layer, lined, (main, rest))
+
+        def step(window, carry):
+            attention_forward(
+                window, qkv, qkvt.at[layer], prob.at[layer], mixedt.at[layer], mixed, (main, rest),
+                region_mask(window) if masked else None,
+            )
+            return carry
+
+        lax.fori_loop(0, 4, step, 0)
+        attended = nn(mixed[...], w_proj[layer]).astype(BF16)
+        middle = (x + attended.astype(F32)).astype(BF16)
+        pre = nn(normalize(middle.astype(F32))[0].astype(BF16), w_in[layer])
+        phi = cumulative(pre)
+        return middle, pre, phi, phi + pre * density(pre)
+
+    def backward(window, layer):
+        attention_backward(
+            window, source.at[layer], qkvt.at[layer], prob.at[layer], mixedt.at[layer], mgrad, grad,
+            w_qkv[layer], w_proj[layer], gradt, sgrad, wgrad, (main24, rest24),
+        )
+
+    def streams(layer):
         bufs_a = [ref.at[layer] for ref in (a_right_in, a_left_in, a_right_sum, a_left_sum)]
         bufs_b = [ref.at[layer] for ref in (b_right_in, b_left_in, b_right_sum, b_left_sum)]
         bufs = (bufs_a, mine.at[layer], other.at[layer], bufs_b, half.at[layer], half_in.at[layer])
-        streams.append(sum_tiles(tiles, bias_out.at[layer], bufs, ring_sems.at[layer], y_sems.at[layer]))
-        streams.append(
-            sum_weights(
-                wtiles, w_out.at[layer], wpart.at[layer], wmid.at[layer], wowned.at[layer],
-                wdone.at[layer], w_sems.at[layer], 8 * layer,
-            )
+        bias_sum = sum_tiles(tiles.at[layer], bias_out.at[layer], bufs, ring_sems.at[layer], y_sems.at[layer])
+        weight_sum = sum_weights(
+            wtiles.at[layer], w_out.at[layer], wpart.at[layer], wmid.at[layer], wowned.at[layer],
+            wdone.at[layer], w_sems.at[layer], 8 * layer,
         )
-    drain(streams[::2], streams[1::2], (0, 2, 5, 7))
-
-
-def sum_all(tiles0, tiles1, wtiles0, wtiles1):
+        return bias_sum, weight_sum
+
+    cot = nn(load_ref[...], cot_ref[...].reshape(TOK, C)).astype(BF16)
+    sent[0] = nn(send_ref[...], cot).astype(BF16)
+    pl.semaphore_wait(barrier, 32)
+    cot_copies = halo(sent.at[0], arrived.at[0], -1, halo_sems.at[0, 0], halo_sems.at[0, 1])
+    cot = nn(own_ref[...], cot)
+
+    x0 = nn(load_ref[...], tok_ref[...].reshape(TOK, C))
+    x0_s[...] = x0.astype(BF16)
+    middle, pre, phi, slope = forward(x0, 0, False)
+    mid_s[...] = middle
+    slope_s[...] = slope
+    x1 = (middle.astype(F32) + nt((pre * phi).astype(BF16), w_outt[0])).astype(BF16)
+    sent[1] = nn(send_ref[...], x1).astype(BF16)
+    x1_copies = halo(sent.at[1], arrived.at[1], -1, halo_sems.at[1, 0], halo_sems.at[1, 1])
+    x1 = nn(own_ref[...], x1)
+
+    wait_all(x1_copies)
+    x1 = x1 + nn(recv_ref[...], arrived[1])
+    middle, pre, phi, slope = forward(x1, 1, True)
+    wait_all(cot_copies)
+    cot = (cot + nn(recv_ref[...], arrived[0])).astype(BF16)
+    mgrad[...] = mlp_back(middle, cot, slope, w_in[1], w_outt[1])
+    grad[...] = nt(mgrad[...], w_proj[1]).astype(BF16)
+    wgrad[...] = jnp.zeros_like(wgrad)
+
+    def back(window, carry):
+        backward(window, 1)
+        return carry
+
+    lax.fori_loop(0, 4, back, 0)
+    result = (mgrad[...].astype(F32) + norm_back(x1, sgrad[...].astype(F32))).astype(BF16)
+    sent[2] = nn(recvt_ref[...], result).astype(BF16)
+    back_copies = halo(sent.at[2], arrived.at[2], 1, halo_sems.at[2, 0], halo_sems.at[2, 1])
+    upstream = nn(ownt_ref[...], result)
+    pack_bias(main24, rest24, tiles.at[1])
+    pack_weights(wgrad, wtiles.at[1])
+    bias1, weight1 = streams(1)
+    advance(bias1, weight1)
+
+    wait_all(back_copies)
+    upstream = (upstream + nn(sendt_ref[...], arrived[2])).astype(BF16)
+    mgrad[...] = mlp_back(mid_s[...], upstream, slope_s[...], w_in[0], w_outt[0])
+    advance(bias1, weight1)
+    grad[...] = nt(mgrad[...], w_proj[0]).astype(BF16)
+    wgrad[...] = jnp.zeros_like(wgrad)
+    for window in range(4):
+        backward(window, 0)
+        advance(bias1, weight1)
+    pack_bias(main24, rest24, tiles.at[0])
+    pack_weights(wgrad, wtiles.at[0])
+    bias0, weight0 = streams(0)
+    advance(bias0, weight0, bias1)
+    result = (mgrad[...].astype(F32) + norm_back(x0_s[...].astype(F32), sgrad[...].astype(F32))).astype(BF16)
+    grid_out[...] = nn(loadt_ref[...], result).astype(BF16).reshape(144, 4, C)
+    drain([bias1, bias0], [weight1, weight0], (0, 2, 5, 7))
+
+
+def run(tokens, cotangent, matrices, params, bias):
     vmem, dma = pltpu.VMEM, pltpu.SemaphoreType.DMA
 
     def ring(rows):
         return [vmem((2, n, rows, 128), BF16) for n in (4, 3, 4, 3)]
 
+    tok = vmem((TOK, C), BF16)
+    scratch = [
+        tok,
+        vmem((2, TOK, C), BF16),
+        vmem((TOK, 3 * C), BF16),
+        vmem((2, 4, 3 * C, WIN), BF16),
+        vmem((2, 24, WIN, WIN), BF16),
+        vmem((2, 4, C, WIN), BF16),
+        tok,
+        tok,
+        vmem((TOK, FF), F32),
+        tok,
+        tok,
+        vmem((3 * C, WIN), BF16),
+        tok,
+        vmem((C, FF), F32),
+        vmem((WIN * 24, 128), F32),
+        vmem((WIN * 24, 128), F32),
+        vmem((72, 72, 128), F32),
+        vmem((4 * WIN * 8 + 8, 128), F32),
+        vmem((4 * WIN * 8 + 8, 128), F32),
+        vmem((2, ROWS, 128), BF16),
+        vmem((2, 80, 16, 128), BF16),
+        vmem((3, SEND, C), BF16),
+        vmem((3, SEND, C), BF16),
+        dma((3, 2, 3)),
+        *ring(256),
+        vmem((2, 256, 128), BF16),
+        vmem((2, 256, 128), BF16),
+        *ring(128),
+        vmem((2, 1024, 128), BF16),
+        vmem((2, 1024, 128), BF16),
+        dma((2, 2, 8, 4)),
+        dma((2, 2, 10)),
+        vmem((2, 16, 5, 16, 128), BF16),
+        vmem((2, 5, 16, 128), BF16),
+        vmem((2, 16, 16, 128), BF16),
+        vmem((2, 5, 16, 128), BF16),
+        dma((2, 8, 16)),
+    ]
+    operands = [tokens, cotangent, *matrices, *params, bias]
     return pl.pallas_call(
-        sum_kernel,
+        kernel,
         out_shape=[
+            jax.ShapeDtypeStruct((144, 4, C), BF16),
             jax.ShapeDtypeStruct((2, ROWS, 128), BF16),
             jax.ShapeDtypeStruct((2, 80, 16, 128), BF16),
         ],
-        in_specs=[pl.BlockSpec(memory_space=vmem)] * 4,
-        out_specs=[pl.BlockSpec(memory_space=vmem)] * 2,
-        scratch_shapes=[
-            *ring(256),
-            vmem((2, 256, 128), BF16),
-            vmem((2, 256, 128), BF16),
-            *ring(128),
-            vmem((2, 1024, 128), BF16),
-            vmem((2, 1024, 128), BF16),
-            dma((2, 2, 8, 4)),
-            dma((2, 2, 10)),
-            vmem((2, 16, 5, 16, 128), BF16),
-            vmem((2, 5, 16, 128), BF16),
-            vmem((2, 16, 16, 128), BF16),
-            vmem((2, 5, 16, 128), BF16),
-            dma((2, 8, 16)),
-        ],
+        in_specs=[pl.BlockSpec(memory_space=vmem)] * len(operands),
+        out_specs=[pl.BlockSpec(memory_space=vmem)] * 3,
+        scratch_shapes=scratch,
         compiler_params=pltpu.CompilerParams(
-            collective_id=2, has_side_effects=True, vmem_limit_bytes=VMEM_LIMIT
+            collective_id=0, has_side_effects=True, vmem_limit_bytes=VMEM_LIMIT
         ),
-    )(tiles0, tiles1, wtiles0, wtiles1)
+    )(*operands)
 
 
 def unpack_kernel(tiles_ref, wtiles_ref, bias_out, qkv_out, proj_out):
@@ -733,37 +708,9 @@
 
 def shards(tokens, cotangent, w_qkv, w_proj, w_in, w_out, earth_bias):
     load, own, send, recv = _matrices()
-    loadt, ownt, recvt, sendt = (jnp.asarray(m.T, BF16) for m in (load, own, recv, send))
-    load, own, send, recv = (jnp.asarray(m, BF16) for m in (load, own, send, recv))
+    matrices = [jnp.asarray(m, BF16) for m in (load, own, send, recv, load.T, own.T, recv.T, send.T)]
     params = [w_qkv, w_proj, w_in, w_out.transpose(0, 2, 1)]
-    tok, wide = ((TOK, C), BF16), ((TOK, 3 * C), BF16)
-    qkvt, mixedt = ((4, 3 * C, WIN), BF16), ((4, C, WIN), BF16)
-    prob = ((24, WIN, WIN), BF16)
-    spread = [((4 * WIN * 8 + 8, 128), F32)] * 2 + [((72, 72, 128), F32)]
-    back = [tok, tok, ((3 * C, WIN), BF16), tok, ((C, FF), F32), ((WIN * 24, 128), F32), ((WIN * 24, 128), F32)]
-    sums = [((256, 16, 128), BF16), ((80, 16, 128), BF16)]
-
-    *state, kept, sent = compute_call(
-        forward_kernel,
-        [to_cells(tokens), to_cells(cotangent), load, own, send] + [(p, 0) for p in params + [earth_bias]],
-        [tok, tok, qkvt, prob, mixedt, tok, ((TOK, FF), BF16), ((2, TOK, C), BF16), ((2, SEND, C), BF16)],
-        [wide, tok] + spread,
-    )
-    arrived = exchange(sent, -1, 0)
-    kept, sent, tiles1, wtiles1 = compute_call(
-        middle_kernel,
-        [kept, arrived, recv, ownt, recvt] + [(p, 1) for p in params + [earth_bias]],
-        [tok, ((1, SEND, C), BF16)] + sums,
-        [tok, wide, qkvt, prob, mixedt, tok] + back + spread,
-    )
-    arrived = exchange(sent, 1, 1)
-    grid, tiles0, wtiles0 = compute_call(
-        backward_kernel,
-        [kept, arrived, sendt, loadt] + state + [(p, 0) for p in params],
-        [((144, 4, C), BF16)] + sums,
-        back,
-    )
-    tiles, wtiles = sum_all(tiles0.reshape(ROWS, 128), tiles1.reshape(ROWS, 128), wtiles0, wtiles1)
+    grid, tiles, wtiles = run(to_cells(tokens), to_cells(cotangent), matrices, params, earth_bias)
     bias_grad, qkv_grad, proj_grad = unpack(tiles, wtiles)
     grid = grid.reshape(12, 12, 4, C).transpose(2, 0, 1, 3)
     return grid, qkv_grad, proj_grad, bias_grad

time: 175 us -> 161 us (0.920)
  Pallas kernels: 165 us -> 149 us
    pallas_call x6 -> x1, Pallas kernels: 160 us -> 145 us  [run(): pl.pallas_call(kernel, out_shape=[jax.ShapeDtypeStruct((144, 4, C), BF16)...]
    unnamed x2 -> x5, local copies, waits for them, and re-layouts: 9.81 us -> 10.6 us
where the time goes in v4:
time: 161 us
  Pallas kernels  149 us (93%)
  local copies, waits for them, and re-layouts  10.6 us (7%)
    pallas_call x1, Pallas kernels, run(): pl.pallas_call(kernel, out_shape=[jax.ShapeDtypeStruct((144, 4, C), BF16)...  145 us
    unnamed x5, local copies, waits for them, and re-layouts  10.6 us
    pallas_call x1, Pallas kernels, unpack(): pl.pallas_call(unpack_kernel, grid=(2,), out_shape=[jax.ShapeDtypeStruct(...  4.45 us

profile of v4, /device:TPU:8, one launch (start us, length us, event | category | flops | bytes accessed | tf_op | source)
XLA Modules:
  0.0 160.6 jit_solution(16982105504609391045)
XLA Ops:
  0.6 3.3 %copy.19.bias_ref = bf16[2,2,2,6,20736]{4,3,2,1,0:T(8,128)(2,1)} copy(bf16[2,2,2,6,20736]{4,2,3,1,0:T(2,128)(2,1)} %param.21) | data formatting | bytes 3981312 | tf_op args[6]
  3.9 144.9 %shard_map.174 = (bf16[144,4,192]{2,1,0:T(4,128)(2,1)}, bf16[2,4096,128]{2,1,0:T(8,128)(2,1)}, bf16[2,80,16,128]{3,2,1,0:T(8,128)(2,1)}) custom-call(bf16[144,4,192]{2,1,0:T(4,128)(2,1)} %bitcast.11, bf16[144,4,192]{2,1,0:T(4,128)(2,1)} %bitcast.12, bf16[576,576]{1,0:T(8,128)(2,1)} %constant.16.clone.load_ref, bf16[576,576]{1,0:T(8,128)(2,1)} %constant.17.clone.own_ref, ...), custom_call_target="tpu_custom_call" | custom-call | tf_op jit(solution)/shard_map/pallas_call | solution.py:653
  148.9 4.5 %shard_map.175 = (f32[2,2,2,6,20736]{4,3,2,1,0:T(8,128)}, f32[2,192,576]{2,1,0:T(8,128)}, f32[2,192,192]{2,1,0:T(8,128)}) custom-call(bf16[2,4096,128]{2,1,0:T(8,128)(2,1)} %get-tuple-element.11.tiles_ref, bf16[2,80,16,128]{3,2,1,0:T(8,128)(2,1)} %get-tuple-element.12.wtiles_ref), custom_call_target="tpu_custom_call" | custom-call | tf_op jit(solution)/shard_map/pallas_call | solution.py:684
  153.3 0.0 copy-start
  153.3 6.5 %copy.20 = f32[2,2,2,6,20736]{4,2,3,1,0:T(2,128)} copy(f32[2,2,2,6,20736]{4,3,2,1,0:T(8,128)} %get-tuple-element.19) | data formatting | bytes 7962624
  159.9 0.0 copy-done
  159.9 0.7 copy.22
Async XLA Ops:
  153.3 6.5 %copy-start = (bf16[144,4,192]{2,1,0:T(4,128)(2,1)S(1)}, bf16[144,4,192]{2,1,0:T(4,128)(2,1)}, u32[]{:S(2)}) copy-start(bf16[144,4,192]{2,1,0:T(4,128)(2,1)} %get-tuple-element.10) | copy-start | bytes 663556

commit v5 on v4

--- a/solution.py
+++ b/solution.py
@@ -588,12 +588,13 @@
     wait_all(back_copies)
     upstream = (upstream + nn(sendt_ref[...], arrived[2])).astype(BF16)
     mgrad[...] = mlp_back(mid_s[...], upstream, slope_s[...], w_in[0], w_outt[0])
-    advance(bias1, weight1)
     grad[...] = nt(mgrad[...], w_proj[0]).astype(BF16)
     wgrad[...] = jnp.zeros_like(wgrad)
     for window in range(4):
         backward(window, 0)
-        advance(bias1, weight1)
+        if window % 2 == 0:
+            advance(bias1)
+    advance(weight1)
     pack_bias(main24, rest24, tiles.at[0])
     pack_weights(wgrad, wtiles.at[0])
     bias0, weight0 = streams(0)

time: 161 us -> 150 us (0.932)
  Pallas kernels: 149 us -> 137 us
    pallas_call x1, Pallas kernels: 145 us -> 133 us  [run(): pl.pallas_call(kernel, out_shape=[jax.ShapeDtypeStruct((144, 4, C), BF16)...]
where the time goes in v5:
time: 150 us; the launch traced here: 148 us
  Pallas kernels  137 us (91%)
  local copies, waits for them, and re-layouts  10.6 us (7%)
    pallas_call x1, Pallas kernels, run(): pl.pallas_call(kernel, out_shape=[jax.ShapeDtypeStruct((144, 4, C), BF16)...  133 us
    unnamed x5, local copies, waits for them, and re-layouts  10.6 us
    pallas_call x1, Pallas kernels, unpack(): pl.pallas_call(unpack_kernel, grid=(2,), out_shape=[jax.ShapeDtypeStruct(...  4.45 us

profile of v5, /device:TPU:8, one launch (start us, length us, event | category | flops | bytes accessed | tf_op | source)
XLA Modules:
  0.0 148.2 jit_solution(12065438341542733665)
XLA Ops:
  0.6 3.3 %copy.19.bias_ref = bf16[2,2,2,6,20736]{4,3,2,1,0:T(8,128)(2,1)} copy(bf16[2,2,2,6,20736]{4,2,3,1,0:T(2,128)(2,1)} %param.21) | data formatting | bytes 3981312 | tf_op args[6]
  3.9 132.6 %shard_map.174 = (bf16[144,4,192]{2,1,0:T(4,128)(2,1)}, bf16[2,4096,128]{2,1,0:T(8,128)(2,1)}, bf16[2,80,16,128]{3,2,1,0:T(8,128)(2,1)}) custom-call(bf16[144,4,192]{2,1,0:T(4,128)(2,1)} %bitcast.11, bf16[144,4,192]{2,1,0:T(4,128)(2,1)} %bitcast.12, bf16[576,576]{1,0:T(8,128)(2,1)} %constant.16.clone.load_ref, bf16[576,576]{1,0:T(8,128)(2,1)} %constant.17.clone.own_ref, ...), custom_call_target="tpu_custom_call" | custom-call | tf_op jit(solution)/shard_map/pallas_call | solution.py:654
  136.5 4.5 %shard_map.175 = (f32[2,2,2,6,20736]{4,3,2,1,0:T(8,128)}, f32[2,192,576]{2,1,0:T(8,128)}, f32[2,192,192]{2,1,0:T(8,128)}) custom-call(bf16[2,4096,128]{2,1,0:T(8,128)(2,1)} %get-tuple-element.11.tiles_ref, bf16[2,80,16,128]{3,2,1,0:T(8,128)(2,1)} %get-tuple-element.12.wtiles_ref), custom_call_target="tpu_custom_call" | custom-call | tf_op jit(solution)/shard_map/pallas_call | solution.py:685
  141.0 0.0 copy-start
  141.0 6.5 %copy.20 = f32[2,2,2,6,20736]{4,2,3,1,0:T(2,128)} copy(f32[2,2,2,6,20736]{4,3,2,1,0:T(8,128)} %get-tuple-element.19) | data formatting | bytes 7962624
  147.5 0.0 copy-done
  147.5 0.7 copy.22
Async XLA Ops:
  141.0 6.5 %copy-start = (bf16[144,4,192]{2,1,0:T(4,128)(2,1)S(1)}, bf16[144,4,192]{2,1,0:T(4,128)(2,1)}, u32[]{:S(2)}) copy-start(bf16[144,4,192]{2,1,0:T(4,128)(2,1)} %get-tuple-element.10) | copy-start | bytes 663556

commit v6 on v4

--- a/solution.py
+++ b/solution.py
@@ -513,7 +513,6 @@
     def forward(x, layer, masked):
         source[layer] = normalize(x)[0].astype(BF16)
         qkv[...] = nn(source[layer], w_qkv[layer]).astype(BF16)
-        spread_bias(bias_ref, layer, lined, (main, rest))
 
         def step(window, carry):
             attention_forward(
@@ -554,6 +553,7 @@
 
     x0 = nn(load_ref[...], tok_ref[...].reshape(TOK, C))
     x0_s[...] = x0.astype(BF16)
+    spread_bias(bias_ref, 0, lined, (main, rest))
     middle, pre, phi, slope = forward(x0, 0, False)
     mid_s[...] = middle
     slope_s[...] = slope
@@ -561,12 +561,13 @@
     sent[1] = nn(send_ref[...], x1).astype(BF16)
     x1_copies = halo(sent.at[1], arrived.at[1], -1, halo_sems.at[1, 0], halo_sems.at[1, 1])
     x1 = nn(own_ref[...], x1)
+    spread_bias(bias_ref, 1, lined, (main, rest))
+    wait_all(cot_copies)
+    cot = (cot + nn(recv_ref[...], arrived[0])).astype(BF16)
 
     wait_all(x1_copies)
     x1 = x1 + nn(recv_ref[...], arrived[1])
     middle, pre, phi, slope = forward(x1, 1, True)
-    wait_all(cot_copies)
-    cot = (cot + nn(recv_ref[...], arrived[0])).astype(BF16)
     mgrad[...] = mlp_back(middle, cot, slope, w_in[1], w_outt[1])
     grad[...] = nt(mgrad[...], w_proj[1]).astype(BF16)
     wgrad[...] = jnp.zeros_like(wgrad)
@@ -585,15 +586,16 @@
     bias1, weight1 = streams(1)
     advance(bias1, weight1)
 
+    advance(bias1)
+    advance(bias1)
     wait_all(back_copies)
     upstream = (upstream + nn(sendt_ref[...], arrived[2])).astype(BF16)
     mgrad[...] = mlp_back(mid_s[...], upstream, slope_s[...], w_in[0], w_outt[0])
-    advance(bias1, weight1)
     grad[...] = nt(mgrad[...], w_proj[0]).astype(BF16)
     wgrad[...] = jnp.zeros_like(wgrad)
     for window in range(4):
         backward(window, 0)
-        advance(bias1, weight1)
+        advance(bias1 if window % 2 == 0 else weight1)
     pack_bias(main24, rest24, tiles.at[0])
     pack_weights(wgrad, wtiles.at[0])
     bias0, weight0 = streams(0)

time: 161 us -> 151 us (0.938)
  Pallas kernels: 149 us -> 139 us
    pallas_call x1, Pallas kernels: 145 us -> 135 us  [run(): pl.pallas_call(kernel, out_shape=[jax.ShapeDtypeStruct((144, 4, C), BF16)...]
where the time goes in v6:
time: 151 us; the launch traced here: 150 us
  Pallas kernels  139 us (92%)
  local copies, waits for them, and re-layouts  10.6 us (7%)
    pallas_call x1, Pallas kernels, run(): pl.pallas_call(kernel, out_shape=[jax.ShapeDtypeStruct((144, 4, C), BF16)...  135 us
    unnamed x5, local copies, waits for them, and re-layouts  10.6 us
    pallas_call x1, Pallas kernels, unpack(): pl.pallas_call(unpack_kernel, grid=(2,), out_shape=[jax.ShapeDtypeStruct(...  4.41 us

profile of v6, /device:TPU:8, one launch (start us, length us, event | category | flops | bytes accessed | tf_op | source)
XLA Modules:
  0.0 150.3 jit_solution(6575587552988967045)
XLA Ops:
  0.6 3.3 %copy.19.bias_ref = bf16[2,2,2,6,20736]{4,3,2,1,0:T(8,128)(2,1)} copy(bf16[2,2,2,6,20736]{4,2,3,1,0:T(2,128)(2,1)} %param.21) | data formatting | bytes 3981312 | tf_op args[6]
  3.9 134.7 %shard_map.174 = (bf16[144,4,192]{2,1,0:T(4,128)(2,1)}, bf16[2,4096,128]{2,1,0:T(8,128)(2,1)}, bf16[2,80,16,128]{3,2,1,0:T(8,128)(2,1)}) custom-call(bf16[144,4,192]{2,1,0:T(4,128)(2,1)} %bitcast.11, bf16[144,4,192]{2,1,0:T(4,128)(2,1)} %bitcast.12, bf16[576,576]{1,0:T(8,128)(2,1)} %constant.16.clone.load_ref, bf16[576,576]{1,0:T(8,128)(2,1)} %constant.17.clone.own_ref, ...), custom_call_target="tpu_custom_call" | custom-call | tf_op jit(solution)/shard_map/pallas_call | solution.py:655
  138.7 4.4 %shard_map.175 = (f32[2,2,2,6,20736]{4,3,2,1,0:T(8,128)}, f32[2,192,576]{2,1,0:T(8,128)}, f32[2,192,192]{2,1,0:T(8,128)}) custom-call(bf16[2,4096,128]{2,1,0:T(8,128)(2,1)} %get-tuple-element.11.tiles_ref, bf16[2,80,16,128]{3,2,1,0:T(8,128)(2,1)} %get-tuple-element.12.wtiles_ref), custom_call_target="tpu_custom_call" | custom-call | tf_op jit(solution)/shard_map/pallas_call | solution.py:686
  143.1 0.0 copy-start
  143.1 6.5 %copy.20 = f32[2,2,2,6,20736]{4,2,3,1,0:T(2,128)} copy(f32[2,2,2,6,20736]{4,3,2,1,0:T(8,128)} %get-tuple-element.19) | data formatting | bytes 7962624
  149.6 0.0 copy-done
  149.6 0.7 copy.22
Async XLA Ops:
  143.1 6.5 %copy-start = (bf16[144,4,192]{2,1,0:T(4,128)(2,1)S(1)}, bf16[144,4,192]{2,1,0:T(4,128)(2,1)}, u32[]{:S(2)}) copy-start(bf16[144,4,192]{2,1,0:T(4,128)(2,1)} %get-tuple-element.10) | copy-start | bytes 663556
